TPU v7x, 256 devices: a whole 4x4x8 slice. The times are simulated.
256 devices in a mesh: dp: 16 (over x, z_lo, core), tensor: 16 (over z_hi, y).
Axes of the slice: x: 4, y: 4, z: 8 (z_hi: 4, z_lo: 2; z = z_hi * 2 + z_lo), core: 2. Of those that a mesh axis runs over, the one named last changes fastest.
Arguments:
- tokens_in: bfloat16 [6144, 8192], P('dp', 'tensor'), may hold values from -21 to 21
- out_grad: bfloat16 [6144, 8192], P('dp', 'tensor'), may hold values from -6 to 6
- q_weight: bfloat16 [8192, 8192], P('dp', 'tensor'), may hold values from -0.0625 to 0.0625
- kv_weight: bfloat16 [8192, 2048], P('dp', 'tensor'), may hold values from -0.0625 to 0.0625
Outputs:
- input_grad: bfloat16 [6144, 8192], P('dp', 'tensor')
- q_grad: bfloat16 [8192, 8192], P('dp', 'tensor')
- kv_grad: bfloat16 [8192, 2048], P('dp', 'tensor')
All inputs are finite; a program needn't handle non-finite values.
Results may differ from a plain program's by a relative error of at most 0.025.
Values may be sent and summed in bfloat16 or wider, within the bound.
A program may use at most 128 MiB of HBM per device.

v0:
```python
import jax
import jax.numpy as jnp
from jax import lax
from jax.sharding import PartitionSpec as P


def swapped(value, axis, stride):
    mask = 2**stride
    pairs = [(source, source ^ mask) for source in range(lax.axis_size(axis))]
    return lax.ppermute(value, axis, pairs)


def rope_tables(length, size):
    half = size // 2
    positions = jnp.arange(length, dtype=jnp.float32)
    inverse = 500000.0 ** (-(jnp.arange(half, dtype=jnp.float32) * 2.0 / size))
    angle = positions[:, None] * inverse[None, :]
    return (jnp.cos(angle), jnp.sin(angle))


def rotate(value, cosine, sine):
    half = value.shape[-1] // 2
    first = value[..., :half]
    second = value[..., half:]
    return jnp.concatenate(
        [first * cosine - second * sine, second * cosine + first * sine], axis=-1
    )


def body(tokens_in, out_grad, q_weight, kv_weight):
    x_full = lax.all_gather(tokens_in, "tensor", axis=1, tiled=True)
    wq_full, wkv_full = (
        lax.all_gather(q_weight, "dp", axis=0, tiled=True),
        lax.all_gather(kv_weight, "dp", axis=0, tiled=True),
    )
    length = x_full.shape[0]
    head_size = wkv_full.shape[1]
    local_heads = wq_full.shape[1] // head_size
    scale = head_size ** (-0.5)
    is_even = lax.axis_index("tensor") % 2 == 0
    cosine, sine = rope_tables(length, head_size)
    cos_h = cosine[:, None, :]
    sin_h = sine[:, None, :]
    q_proj = jnp.dot(x_full, wq_full, preferred_element_type=jnp.float32).reshape(
        length, local_heads, head_size
    )
    queries = rotate(q_proj, cos_h, sin_h).astype(jnp.bfloat16)
    partner_cols = swapped(wkv_full, "tensor", 0)
    key_cols = jnp.where(is_even, wkv_full, partner_cols)
    value_cols = jnp.where(is_even, partner_cols, wkv_full)
    keys = rotate(
        jnp.dot(x_full, key_cols, preferred_element_type=jnp.float32), cosine, sine
    ).astype(jnp.bfloat16)
    values = jnp.dot(x_full, value_cols, preferred_element_type=jnp.float32).astype(jnp.bfloat16)
    key_float = keys.astype(jnp.float32)
    value_float = values.astype(jnp.float32)
    q_float = queries.astype(jnp.float32)
    scores = jnp.einsum("shd,td->hst", q_float, key_float) * scale
    causal = jnp.arange(length)[None, :] <= jnp.arange(length)[:, None]
    scores = jnp.where(causal[None], scores, -jnp.inf)
    top = jnp.max(scores, axis=-1, keepdims=True)
    expo = jnp.exp(scores - top)
    probs = expo / jnp.sum(expo, axis=-1, keepdims=True)
    probs_low = lax.optimization_barrier(probs.astype(jnp.bfloat16)).astype(jnp.float32)
    grad_float = out_grad.reshape(length, local_heads, head_size).astype(jnp.float32)
    dprobs = jnp.einsum("shd,td->hst", grad_float, value_float)
    delta = jnp.sum(probs * dprobs, axis=-1, keepdims=True)
    dscores = lax.optimization_barrier(
        (probs * (dprobs - delta) * scale).astype(jnp.bfloat16)
    ).astype(jnp.float32)
    dq = jnp.einsum("hst,td->shd", dscores, key_float)
    dq = rotate(dq, cos_h, -sin_h).astype(jnp.bfloat16).reshape(length, local_heads * head_size)
    key_part = jnp.einsum("hst,shd->td", dscores, q_float)
    value_part = jnp.einsum("hst,shd->td", probs_low, grad_float)
    outgoing = jnp.where(is_even, value_part, key_part)
    incoming = swapped(outgoing, "tensor", 0)
    role_sum = jnp.where(is_even, key_part, value_part) + incoming
    role_grad = jnp.where(is_even, rotate(role_sum, cosine, -sine), role_sum).astype(jnp.bfloat16)
    grads = jnp.concatenate([dq, role_grad], axis=1)
    weight_sums = lax.psum_scatter(
        lax.dot_general(
            x_full, grads, (((0,), (0,)), ((), ())), preferred_element_type=jnp.float32
        ).astype(jnp.bfloat16),
        "dp",
        scatter_dimension=0,
        tiled=True,
    ).astype(jnp.float32)
    q_grad = weight_sums[:, : local_heads * head_size].astype(jnp.bfloat16)
    kv_grad = weight_sums[:, local_heads * head_size :].astype(jnp.bfloat16)
    contract = (((1,), (1,)), ((), ()))
    partial_rows = lax.dot_general(dq, wq_full, contract, preferred_element_type=jnp.float32)
    partial_rows = partial_rows + lax.dot_general(
        role_grad, wkv_full, contract, preferred_element_type=jnp.float32
    )
    input_grad = lax.psum_scatter(
        partial_rows.astype(jnp.bfloat16), "tensor", scatter_dimension=1, tiled=True
    )
    return (input_grad, q_grad, kv_grad)


def solution(mesh):
    in_specs = (P("dp", "tensor"), P("dp", "tensor"), P("dp", "tensor"), P("dp", "tensor"))
    out_specs = (P("dp", "tensor"), P("dp", "tensor"), P("dp", "tensor"))
    return jax.shard_map(body, mesh=mesh, in_specs=in_specs, out_specs=out_specs, check_vma=False)
```

profile of v0, /device:TPU:1, one launch (start us, length us, event | category | flops | bytes accessed | tf_op | source)
XLA Modules:
  0.0 496.6 jit_solution(11741360693696178806)
XLA Ops:
  9.4 41.3 %all-gather.4.cloned.1.call-done = bf16[8192,128]{1,0:T(8,128)(2,1)} async-done(((bf16[512,128]{1,0:T(8,128)(2,1)}), bf16[8192,128]{1,0:T(8,128)(2,1)}) %all-gather.4.cloned.1.call-update) | async-done | bytes 2097168 | tf_op jit(solution)/shard_map/all_gather | solution.py:34
  50.7 1.2 collective-permute-start
  51.9 1.2 copy.48
  53.8 54.7 %collective-permute-done = bf16[8192,128]{1,0:T(8,128)(2,1)S(1)} collective-permute-done((bf16[8192,128]{1,0:T(8,128)(2,1)}, bf16[8192,128]{1,0:T(8,128)(2,1)S(1)}, u32[]{:S(2)}, u32[]{:S(2)}) %collective-permute-start) | collective-permute-done | bytes 2097184 | tf_op jit(solution)/shard_map/ppermute | solution.py:10
  108.5 1.3 copy-done.1
  109.8 47.3 %all-gather.6.cloned.1.call-done = bf16[384,8192]{1,0:T(8,128)(2,1)} async-done(((bf16[384,512]{1,0:T(8,128)(2,1)}), bf16[384,8192]{1,0:T(8,128)(2,1)}) %all-gather.6.cloned.1.call-update) | async-done | bytes 6291472 | tf_op jit(solution)/shard_map/all_gather | solution.py:31
  157.1 5.5 %fusion.16 = f32[384,128]{0,1:T(8,128)S(1)} fusion(bf16[384,8192]{1,0:T(8,128)(2,1)} %all-gather.6.cloned.1.call-done, bf16[8192,128]{1,0:T(8,128)(2,1)} %all-gather.4.cloned.1.call-done, bf16[8192,128]{1,0:T(8,128)(2,1)} %copy-done.1, pred[]{:T(512)S(6)} %eq.5), kind=kOutput, calls=%fused_computation.24 | convolution fusion | flops 806354944 | bytes 10682369 | tf_op jit(solution)/shard_map/dot_general | solution.py:52
  162.7 1.1 fusion.37
  165.5 7.6 %fusion.26 = f32[384,384,4]{1,0,2:T(8,128)} fusion(bf16[384,4,128]{0,2,1:T(8,128)(2,1)S(1)} %bitcast.60, bf16[384,8192]{1,0:T(8,128)(2,1)} %all-gather.6.cloned.1.call-done, bf16[8192,128]{1,0:T(8,128)(2,1)} %copy-done.1, bf16[8192,128]{1,0:T(8,128)(2,1)S(1)} %copy-done, pred[]{:T(512)S(6)} %eq.5), kind=kOutput, calls=%fused_computation.29 | convolution fusion | flops 957399040 | bytes 13238273 | tf_op jit(solution)/shard_map/shd,td->hst/dot_general | solution.py:66
  173.1 39.5 %all-gather.8.cloned.1.call-done = bf16[8192,512]{1,0:T(8,128)(2,1)} async-done(((bf16[512,512]{1,0:T(8,128)(2,1)}), bf16[8192,512]{1,0:T(8,128)(2,1)}) %all-gather.8.cloned.1.call-update) | async-done | bytes 8388624 | tf_op jit(solution)/shard_map/all_gather | solution.py:33
  212.5 9.5 %fusion.49 = f32[384,512]{1,0:T(8,128)} fusion(bf16[384,8192]{1,0:T(8,128)(2,1)} %all-gather.6.cloned.1.call-done, bf16[8192,512]{1,0:T(8,128)(2,1)} %all-gather.8.cloned.1.call-done), kind=kOutput, calls=%fused_computation.66 | convolution fusion | flops 3221225472 | bytes 15466496 | tf_op jit(solution)/shard_map/dot_general | solution.py:44
  222.0 1.4 reshape.87
  225.3 3.5 fusion.48
  228.8 2.0 fusion.46
  231.1 3.1 fusion.5
  235.5 1.3 broadcast_select_fusion
  236.7 1.2 collective-permute-start.1
  238.8 4.5 collective-permute-done.1
  244.8 11.2 %fusion.2 = bf16[8192,640]{0,1:T(8,128)(2,1)} fusion(bf16[384,8192]{1,0:T(8,128)(2,1)} %all-gather.6.cloned.1.call-done, bf16[384,128]{0,1:T(8,128)(2,1)S(1)} %fusion.34, bf16[384,512]{0,1:T(8,128)(2,1)S(1)} %bitcast.62), kind=kOutput, calls=%fused_computation.4 | convolution fusion | flops 4032757760 | bytes 17268736 | tf_op jit(solution)/shard_map/dot_general | solution.py:81
  256.0 5.9 %fusion.50 = f32[384,8192]{1,0:T(8,128)S(1)} fusion(bf16[384,512]{0,1:T(8,128)(2,1)S(1)} %bitcast.63, bf16[8192,512]{1,0:T(8,128)(2,1)} %all-gather.8.cloned.1.call-done), kind=kOutput, calls=%fused_computation.67 | convolution fusion | flops 3221225472 | bytes 21364736 | tf_op jit(solution)/shard_map/dot_general | solution.py:91
  262.0 4.5 add_convert_fusion
  266.5 110.7 %reduce-scatter.5.cloned.1.call-done = bf16[512,640]{0,1:T(8,128)(2,1)} async-done(((bf16[8192,640]{0,1:T(8,128)(2,1)}), bf16[512,640]{0,1:T(8,128)(2,1)}) %reduce-scatter.5.cloned.1.call-update) | async-done | bytes 655376 | tf_op jit(solution)/shard_map/reduce_scatter | solution.py:80
  377.2 1.1 slice.50
  380.1 110.0 %reduce-scatter.3.cloned.1.call-done = bf16[384,512]{1,0:T(8,128)(2,1)} async-done(((bf16[384,8192]{1,0:T(8,128)(2,1)}), bf16[384,512]{1,0:T(8,128)(2,1)}) %reduce-scatter.3.cloned.1.call-update) | async-done | bytes 393232 | tf_op jit(solution)/shard_map/reduce_scatter | solution.py:95
  (46 shorter events, 12.2 us)
Async XLA Ops:
  7.2 43.5 %all-gather.4.cloned.1.call-start = ((), (), s32[]{:S(2)}) async-start(), calls=%async_computation.2 | async-start | bytes 2228224 | tf_op jit(solution)/shard_map/all_gather | solution.py:34
  7.9 149.2 %all-gather.6.cloned.1.call-start = ((), (), s32[]{:S(2)}) async-start(), calls=%async_computation.3 | async-start | bytes 6684672 | tf_op jit(solution)/shard_map/all_gather | solution.py:31
  8.6 203.9 %all-gather.8.cloned.1.call-start = ((), (), s32[]{:S(2)}) async-start(), calls=%async_computation.4 | async-start | bytes 8912896 | tf_op jit(solution)/shard_map/all_gather | solution.py:33
  9.4 367.8 %reduce-scatter.5.cloned.1.call-start = ((), (), s32[]{:S(2)}) async-start(), calls=%async_computation.6 | async-start | bytes 11141120 | tf_op jit(solution)/shard_map/reduce_scatter | solution.py:80
  50.7 57.8 %collective-permute-start = (bf16[8192,128]{1,0:T(8,128)(2,1)}, bf16[8192,128]{1,0:T(8,128)(2,1)S(1)}, u32[]{:S(2)}, u32[]{:S(2)}) collective-permute-start(bf16[8192,128]{1,0:T(8,128)(2,1)} %all-gather.4.cloned.1.call-done), channel_id=1, source_target_pairs={{0,1},{1,0},{2,3},{3,2},{4,5},{5,4},{6,7},{7,6},{8,9},{9,8},{10,11... | collective-permute-start | bytes 6291464 | tf_op jit(solution)/shard_map/ppermute | solution.py:10
  108.5 1.3 copy-start.1
  157.1 8.4 %copy-start = (bf16[8192,128]{1,0:T(8,128)(2,1)S(1)}, bf16[8192,128]{1,0:T(8,128)(2,1)}, u32[]{:S(2)}) copy-start(bf16[8192,128]{1,0:T(8,128)(2,1)} %all-gather.4.cloned.1.call-done) | copy-start | bytes 6291460
  223.4 0.9 copy-start.6
  223.9 1.4 copy-start.7
  223.9 1.4 copy-start.8
  228.8 2.4 copy-start.2
  231.1 3.1 copy-start.3
  234.8 3.1 copy-start.5
  236.7 6.6 %copy-start.4 = (f32[384,128]{0,1:T(8,128)S(1)}, f32[384,128]{0,1:T(8,128)}, u32[]{:S(2)}) copy-start(f32[384,128]{0,1:T(8,128)} %get-tuple-element.27) | copy-start | bytes 589828
  236.7 6.6 %collective-permute-start.1 = (f32[384,128]{0,1:T(8,128)}, f32[384,128]{0,1:T(8,128)}, u32[]{:S(2)}, u32[]{:S(2)}) collective-permute-start(f32[384,128]{0,1:T(8,128)} %get-tuple-element.26), channel_id=1, source_target_pairs={{0,1},{1,0},{2,3},{3,2},{4,5},{5,4},{6,7},{7,6},{8,9},{9,8},{10,11... | collective-permute-start | bytes 589832 | tf_op jit(solution)/shard_map/ppermute | solution.py:10
  256.0 234.1 %reduce-scatter.3.cloned.1.call-start = ((), (), s32[]{:S(2)}) async-start(), calls=%async_computation.5 | async-start | bytes 6684672 | tf_op jit(solution)/shard_map/reduce_scatter | solution.py:95
  377.2 2.1 slice-start
Sparse Core Ops, SparseCore 0:
  9.8 40.8 all-gather.3
  53.1 103.9 all-gather.5
  159.0 53.5 all-gather.7
  256.1 121.0 reduce-scatter.4
  381.4 108.6 reduce-scatter.2
where the time goes:
time: 497 us
  waiting for transfers between devices  410 us (82%)
  matrix products  50.2 us (10%)
  between operations  13.9 us (3%)
  local copies, waits for them, and re-layouts  10.1 us (2%)
  other arithmetic  9.86 us (2%)
    reduce_scatter x1, waiting for transfers between devices, body(): lax.psum_scatter(lax.dot_general(x_full, grads, (((0,), (0,)), ((), ())),...  111 us
    reduce_scatter x1, waiting for transfers between devices, body(): lax.psum_scatter(partial_rows.astype(jnp.bfloat16), 'tensor', scatter_dim...  110 us
    ppermute x2, waiting for transfers between devices, swapped(): return lax.ppermute(value, axis, pairs)  59.2 us
    all_gather x1, waiting for transfers between devices, body(): x_full = lax.all_gather(tokens_in, 'tensor', axis=1, tiled=True)  47.3 us
    all_gather x1, waiting for transfers between devices, body(): lax.all_gather(kv_weight, 'dp', axis=0, tiled=True)  41.3 us
    all_gather x1, waiting for transfers between devices, body(): lax.all_gather(q_weight, 'dp', axis=0, tiled=True)  39.5 us
    dot_general x1, matrix products, body(): lax.dot_general(x_full, grads, (((0,), (0,)), ((), ())), preferred_elemen...  11.2 us
  transfers between devices with their start and end apart: 7, of which 7 were waited for; matrix products, arithmetic and copies ran while one was open for 6% of the time, Pallas kernels for 0%

commit v1 on v0

v1 whole, which is shorter than its diff:
```python
import functools
import jax
import jax.numpy as jnp
import numpy as np
from jax import lax
from jax.sharding import PartitionSpec as P
from jax.experimental import pallas as pl
from jax.experimental.pallas import tpu as pltpu

MESH = pl.DeviceIdType.MESH
F32, BF16 = jnp.float32, jnp.bfloat16
TOK, FEAT, HD, HEADS, COLS = 384, 512, 128, 4, 640
HT, HW, HG = TOK // 2, FEAT // 2, COLS // 2
N_SEMS = 192


def rope_tables(length, size):
    half = size // 2
    positions = np.arange(length, dtype=np.float32)
    inverse = np.power(
        np.float32(500000.0), -(np.arange(half, dtype=np.float32) * np.float32(2.0) / np.float32(size))
    ).astype(np.float32)
    angle = (positions[:, None] * inverse[None, :]).astype(np.float32).astype(np.float64)
    cosine, sine = np.cos(angle), np.sin(angle)
    return (
        np.concatenate([cosine, cosine], axis=1).astype(np.float32),
        np.concatenate([-sine, sine], axis=1).astype(np.float32),
    )


def dot_nn(a, b):
    return lax.dot_general(a, b, (((1,), (0,)), ((), ())), preferred_element_type=F32)


def dot_nt(a, b):
    return lax.dot_general(a, b, (((1,), (1,)), ((), ())), preferred_element_type=F32)


def dot_tn(a, b):
    return lax.dot_general(a, b, (((0,), (0,)), ((), ())), preferred_element_type=F32)


def kernel(
    x_in, og_in, wq_in, wkv_in, cos_ref, sin_ref,
    dx_out, qg_out, kvg_out,
    xbuf, wbuf, xsib, og, acc, qbuf, kv, gbuf, gt, part, part_low, part_in,
    dxs, ry_full, ry_half, rz_full, rz_half,
    dws, rx_full, rx_half, rzl,
    local_sem, ss, rs,
):
    dp, tn = lax.axis_index("dp"), lax.axis_index("tensor")
    x, zl, c = dp // 4, (dp // 2) % 2, dp % 2
    zh, y = tn // 4, tn % 4
    role = y % 2
    is_key = role == 0

    def wb(dx, dz, dc):
        return ((x + dx) % 4) * 4 + ((zl + dz) % 2) * 2 + (c + dc) % 2

    def tb(dh, dy):
        return ((zh + dh) % 4) * 4 + (y + dy) % 4

    sib = (wb(0, 0, 1), tn)
    zlp = (wb(0, 1, 0), tn)
    xp, xm = (wb(1, 0, 0), tn), (wb(3, 0, 0), tn)
    yp, ym = (dp, tb(0, 1)), (dp, tb(0, 3))
    zp, zm = (dp, tb(1, 0)), (dp, tb(3, 0))
    mate = (dp, zh * 4 + y + 1 - 2 * role)

    names = {}
    pending = []

    def sem(name):
        return names.setdefault(name, len(names))

    def send(name, src, dst, to):
        k = sem(name)
        copy = pltpu.make_async_remote_copy(
            src_ref=src, dst_ref=dst, send_sem=ss.at[k], recv_sem=rs.at[k],
            device_id=to, device_id_type=MESH,
        )
        copy.start()
        pending.append(copy)

    def recv(name, dst):
        k = sem(name)
        pltpu.make_async_remote_copy(
            src_ref=dst, dst_ref=dst, send_sem=ss.at[k], recv_sem=rs.at[k],
            device_id=sib, device_id_type=MESH,
        ).wait_recv()

    def xs(block, h):
        return xbuf.at[block, pl.ds(h * HT, HT)]

    def ws(block, h):
        return wbuf.at[block, pl.ds(h * HW, HW)]

    own_x, own_w = tn, dp
    loads = [
        pltpu.make_async_copy(x_in, xbuf.at[own_x], local_sem.at[0]),
        pltpu.make_async_copy(wq_in, wbuf.at[own_w, :, pl.ds(0, FEAT)], local_sem.at[1]),
        pltpu.make_async_copy(wkv_in, wbuf.at[own_w, :, pl.ds(FEAT, HD)], local_sem.at[2]),
        pltpu.make_async_copy(og_in, og, local_sem.at[3]),
    ]
    for load in loads:
        load.start()
    barrier = pltpu.get_barrier_semaphore()
    neighbours = (sib, zlp, xp, xm, yp, ym, zp, zm)
    for to in neighbours:
        pl.semaphore_signal(barrier, inc=1, device_id=to, device_id_type=MESH)
    pl.semaphore_wait(barrier, len(neighbours))

    def send_x(name, block, h, to):
        send((name, h), xs(block, h), xs(block, h), to)

    def recv_x(name, block, h):
        recv((name, h), xs(block, h))

    def send_w(name, block, h, to):
        send((name, h), ws(block, h), ws(block, h), to)

    def recv_w(name, block, h):
        recv((name, h), ws(block, h))

    def spread_y(j, h):
        send_x(("yp", j), tb(j, 0), h, yp)
        send_x(("ym", j), tb(j, 0), h, ym)

    loads[0].wait()
    for h in (0, 1):
        send_x("zp", own_x, h, zp)
        send_x("zm", own_x, 1 - h, zm)
        send_x(("yp", 0), own_x, h, yp)
        send_x(("ym", 0), own_x, 1 - h, ym)
    loads[1].wait()
    loads[2].wait()
    for h in (0, 1):
        send_w(("xp", 0), own_w, h, xp)
        send_w(("xm", 0), own_w, 1 - h, xm)
    for h in (0, 1):
        send_w("sib", own_w, h, sib)

    def relay_y(j, which):
        if which == 0:
            recv_x(("yp", j), tb(j, 3), 0)
            send_x(("ypr", j), tb(j, 3), 0, yp)
        else:
            recv_x(("ym", j), tb(j, 1), 1)
            send_x(("ymr", j), tb(j, 1), 1, ym)

    def relay_x(dz, which):
        if which == 0:
            recv_w(("xp", dz), wb(3, dz, 0), 0)
            send_w(("xpr", dz), wb(3, dz, 0), 0, xp)
            send_w(("sxp", dz), wb(3, dz, 0), 0, sib)
        else:
            recv_w(("xm", dz), wb(1, dz, 0), 1)
            send_w(("xmr", dz), wb(1, dz, 0), 1, xm)
            send_w(("sxm", dz), wb(1, dz, 0), 1, sib)

    def rest_x(dz):
        recv_w(("xp", dz), wb(3, dz, 0), 1)
        send_w(("sxp", dz), wb(3, dz, 0), 1, sib)
        recv_w(("xm", dz), wb(1, dz, 0), 0)
        send_w(("sxm", dz), wb(1, dz, 0), 0, sib)

    def far_x(dz):
        recv_w(("xpr", dz), wb(2, dz, 0), 0)
        send_w(("sfar", dz), wb(2, dz, 0), 0, sib)
        recv_w(("xmr", dz), wb(2, dz, 0), 1)
        send_w(("sfar", dz), wb(2, dz, 0), 1, sib)

    def from_zl(h):
        block = wb(0, 1, 0)
        recv_w("zl", block, h)
        send_w(("xp", 1), block, h, xp)
        send_w(("xm", 1), block, h, xm)
        send_w("szl", block, h, sib)

    relay_y(0, 0)
    relay_y(0, 1)
    relay_x(0, 0)
    relay_x(0, 1)
    recv_x("zp", tb(3, 0), 0)
    spread_y(3, 0)
    recv_x("zm", tb(1, 0), 1)
    spread_y(1, 1)
    send_w("zl", own_w, 0, zlp)
    rest_x(0)
    relay_y(3, 0)
    relay_y(1, 1)
    recv_x("zp", tb(3, 0), 1)
    spread_y(3, 1)
    recv_x("zm", tb(1, 0), 0)
    spread_y(1, 0)
    send_w("zl", own_w, 1, zlp)
    send_x("zpr", tb(3, 0), 0, zp)
    send_x("zmr", tb(1, 0), 1, zm)
    far_x(0)
    from_zl(0)
    relay_y(3, 1)
    relay_y(1, 0)
    from_zl(1)
    recv_x("zpr", tb(2, 0), 0)
    spread_y(2, 0)
    recv_x("zmr", tb(2, 0), 1)
    spread_y(2, 1)
    relay_x(1, 0)
    relay_x(1, 1)
    relay_y(2, 0)
    relay_y(2, 1)
    rest_x(1)
    far_x(1)
    for j in (0, 3, 1, 2):
        recv_x(("yp", j), tb(j, 3), 1)
        recv_x(("ym", j), tb(j, 1), 0)
        recv_x(("ypr", j), tb(j, 2), 0)
        recv_x(("ymr", j), tb(j, 2), 1)
    for h in (0, 1):
        recv_w("sib", wb(0, 0, 1), h)
        recv_w("szl", wb(0, 1, 1), h)
        for dz in (0, 1):
            recv_w(("sxp", dz), wb(3, dz, 1), h)
            recv_w(("sxm", dz), wb(1, dz, 1), h)
            recv_w(("sfar", dz), wb(2, dz, 1), h)

    for i in range(8):
        send(("xsib", i), xbuf.at[2 * i + 1 - c], xsib.at[i], sib)

    acc[...] = dot_nn(xbuf[0], wbuf[0])

    def project(b, carry):
        acc[...] += dot_nn(xbuf[b], wbuf[b])
        return carry

    lax.fori_loop(1, 16, project, 0)

    def rot(u, rows=slice(None)):
        return u * cos_ref[rows, :] + pltpu.roll(u, HD // 2, 1) * sin_ref[rows, :]

    def unrot(u, rows=slice(None)):
        return u * cos_ref[rows, :] - pltpu.roll(u, HD // 2, 1) * sin_ref[rows, :]

    raw = acc[:, FEAT:COLS]
    kv[role] = jnp.where(is_key, rot(raw), raw).astype(BF16)
    send("kv", kv.at[role], kv.at[role], mate)
    for h in range(HEADS):
        qbuf[:, h * HD:(h + 1) * HD] = rot(acc[:, h * HD:(h + 1) * HD]).astype(BF16)
    part[...] = jnp.zeros_like(part)
    loads[3].wait()
    recv("kv", kv.at[1 - role])

    scale = HD ** -0.5

    def head(h, carry):
        cols = pl.ds(pl.multiple_of(h * HD, HD), HD)
        for i in range(TOK // HD):
            rows, n = slice(i * HD, (i + 1) * HD), (i + 1) * HD
            q, grad = qbuf[rows, cols], og[rows, cols]
            k, v = kv[0, :n], kv[1, :n]
            scores = dot_nt(q, k) * scale
            q_pos = lax.broadcasted_iota(jnp.int32, (HD, n), 0) + i * HD
            k_pos = lax.broadcasted_iota(jnp.int32, (HD, n), 1)
            scores = jnp.where(k_pos <= q_pos, scores, -jnp.inf)
            expo = jnp.exp(scores - jnp.max(scores, axis=-1, keepdims=True))
            probs = expo / jnp.sum(expo, axis=-1, keepdims=True)
            dprobs = dot_nt(grad, v)
            delta = jnp.sum(probs * dprobs, axis=-1, keepdims=True)
            dscores = (probs * (dprobs - delta) * scale).astype(BF16)
            dq = unrot(dot_nn(dscores, k), rows)
            gbuf[rows, cols] = dq.astype(BF16)
            gt[0, cols, rows] = dq.T.astype(BF16)
            part[0, :n] += dot_tn(dscores, q)
            part[1, :n] += dot_tn(probs.astype(BF16), grad)
        return carry

    lax.fori_loop(0, HEADS, head, 0)

    part_low[...] = part[1 - role].astype(BF16)
    send("part", part_low, part_in, mate)
    send("gt_q", gt.at[0, pl.ds(0, FEAT)], gt.at[1, pl.ds(0, FEAT)], sib)
    recv("part", part_in)
    total = part[role] + part_in[...].astype(F32)
    total = jnp.where(is_key, unrot(total), total)
    gbuf[:, FEAT:COLS] = total.astype(BF16)
    gt[0, FEAT:COLS, :] = total.T.astype(BF16)
    send("gt_kv", gt.at[0, pl.ds(FEAT, HD)], gt.at[1, pl.ds(FEAT, HD)], sib)
    for i in range(8):
        recv(("xsib", i), xsib.at[i])

    def dx_half(j, dy, h):
        return dot_nt(gbuf[h * HT:(h + 1) * HT, :], wbuf[tb(j, dy)])

    def dw_half(ddx, dz, h):
        b = wb(ddx, dz, 0)
        rows = slice(h * HG, (h + 1) * HG)
        return dot_nn(gt[0, rows, :], xbuf[b]) + dot_nn(gt[1, rows, :], xsib[b // 2])

    def tslot(ref, i, h):
        return ref.at[i, pl.ds(h * HT, HT)]

    def gslot(ref, i, h):
        return ref.at[i, pl.ds(h * HG, HG)]

    def load_t(ref, i, h):
        return ref[i, h * HT:(h + 1) * HT, :].astype(F32)

    def load_g(ref, i, h):
        return ref[i, h * HG:(h + 1) * HG, :].astype(F32)

    def put_dx(name, j, dy, h, value, dst, to):
        i = j * 4 + dy
        dxs[i, h * HT:(h + 1) * HT, :] = value.astype(BF16)
        send(name, tslot(dxs, i, h), dst, to)

    def put_dw(name, ddx, dz, h, value, dst, to):
        i = ddx * 2 + dz
        dws[i, h * HG:(h + 1) * HG, :] = value.astype(BF16)
        send(name, gslot(dws, i, h), dst, to)

    def s1(j):
        put_dx(("s1", j, 0), j, 2, 0, dx_half(j, 2, 0), ry_half.at[j * 2], yp)
        put_dx(("s1", j, 1), j, 2, 1, dx_half(j, 2, 1), ry_half.at[j * 2 + 1], ym)

    def s2n(j):
        put_dx(("s2", j, 0, 1), j, 1, 1, dx_half(j, 1, 1), tslot(ry_full, j * 2, 1), yp)
        put_dx(("s2", j, 1, 0), j, 3, 0, dx_half(j, 3, 0), tslot(ry_full, j * 2 + 1, 0), ym)

    def s2d(j):
        mine = dx_half(j, 1, 0)
        recv(("s1", j, 0), ry_half.at[j * 2])
        put_dx(("s2", j, 0, 0), j, 1, 0, mine + ry_half[j * 2].astype(F32), tslot(ry_full, j * 2, 0), yp)
        mine = dx_half(j, 3, 1)
        recv(("s1", j, 1), ry_half.at[j * 2 + 1])
        put_dx(
            ("s2", j, 1, 1), j, 3, 1, mine + ry_half[j * 2 + 1].astype(F32), tslot(ry_full, j * 2 + 1, 1), ym
        )

    def s3(j):
        for h in ((1, 0) if j == 1 else (0, 1)):
            mine = dx_half(j, 0, h)
            recv(("s2", j, 0, h), tslot(ry_full, j * 2, h))
            recv(("s2", j, 1, h), tslot(ry_full, j * 2 + 1, h))
            mine = mine + load_t(ry_full, j * 2, h) + load_t(ry_full, j * 2 + 1, h)
            if j == 2:
                put_dx(("z1", h), 2, 0, h, mine, rz_half.at[h], zp if h == 0 else zm)
            elif j == 0:
                recv(("z2", 0, h), tslot(rz_full, 0, h))
                recv(("z2", 1, h), tslot(rz_full, 1, h))
                mine = mine + load_t(rz_full, 0, h) + load_t(rz_full, 1, h)
                dx_out[h * HT:(h + 1) * HT, :] = mine.astype(BF16)
            else:
                side = 0 if j == 1 else 1
                if h == side:
                    recv(("z1", side), rz_half.at[side])
                    mine = mine + rz_half[side].astype(F32)
                put_dx(("z2", side, h), j, 0, h, mine, tslot(rz_full, side, h), zp if j == 1 else zm)

    def t1(dz):
        put_dw(("t1", dz, 0), 2, dz, 0, dw_half(2, dz, 0), rx_half.at[dz * 2], xp)
        put_dw(("t1", dz, 1), 2, dz, 1, dw_half(2, dz, 1), rx_half.at[dz * 2 + 1], xm)

    def t2n(dz):
        put_dw(("t2", dz, 0, 1), 1, dz, 1, dw_half(1, dz, 1), gslot(rx_full, dz * 2, 1), xp)
        put_dw(("t2", dz, 1, 0), 3, dz, 0, dw_half(3, dz, 0), gslot(rx_full, dz * 2 + 1, 0), xm)

    def t2d(dz):
        mine = dw_half(1, dz, 0)
        recv(("t1", dz, 0), rx_half.at[dz * 2])
        put_dw(("t2", dz, 0, 0), 1, dz, 0, mine + rx_half[dz * 2].astype(F32), gslot(rx_full, dz * 2, 0), xp)
        mine = dw_half(3, dz, 1)
        recv(("t1", dz, 1), rx_half.at[dz * 2 + 1])
        put_dw(
            ("t2", dz, 1, 1), 3, dz, 1, mine + rx_half[dz * 2 + 1].astype(F32), gslot(rx_full, dz * 2 + 1, 1), xm
        )

    def t3(dz):
        for h in (0, 1):
            mine = dw_half(0, dz, h)
            recv(("t2", dz, 0, h), gslot(rx_full, dz * 2, h))
            recv(("t2", dz, 1, h), gslot(rx_full, dz * 2 + 1, h))
            mine = mine + load_g(rx_full, dz * 2, h) + load_g(rx_full, dz * 2 + 1, h)
            if dz == 1:
                put_dw(("t3", h), 0, 1, h, mine, rzl.at[pl.ds(h * HG, HG)], zlp)
            else:
                recv(("t3", h), rzl.at[pl.ds(h * HG, HG)])
                mine = (mine + rzl[h * HG:(h + 1) * HG, :].astype(F32)).T.astype(BF16)
                if h == 0:
                    qg_out[:, :HG] = mine
                else:
                    qg_out[:, HG:] = mine[:, :FEAT - HG]
                    kvg_out[...] = mine[:, FEAT - HG:]

    s1(2)
    recv("gt_q", gt.at[1, pl.ds(0, FEAT)])
    recv("gt_kv", gt.at[1, pl.ds(FEAT, HD)])
    t1(1)
    s2n(2)
    s1(1)
    t2n(1)
    s2d(2)
    s2n(1)
    t1(0)
    s1(3)
    s3(2)
    s2d(1)
    t2d(1)
    s2n(3)
    s1(0)
    t2n(0)
    s3(1)
    s2d(3)
    t3(1)
    s2n(0)
    t2d(0)
    s3(3)
    s2d(0)
    t3(0)
    s3(0)

    for copy in pending:
        copy.wait_send()
    assert len(names) <= N_SEMS


def body(tokens_in, out_grad, q_weight, kv_weight):
    cosine, sine = rope_tables(TOK, HD)
    vmem = pl.BlockSpec(memory_space=pltpu.VMEM)
    anywhere = pl.BlockSpec(memory_space=pl.ANY)
    return pl.pallas_call(
        kernel,
        out_shape=(
            jax.ShapeDtypeStruct((TOK, FEAT), BF16),
            jax.ShapeDtypeStruct((FEAT, FEAT), BF16),
            jax.ShapeDtypeStruct((FEAT, HD), BF16),
        ),
        in_specs=[anywhere] * 4 + [vmem] * 2,
        out_specs=(vmem, vmem, vmem),
        scratch_shapes=[
            pltpu.VMEM((16, TOK, FEAT), BF16),
            pltpu.VMEM((16, FEAT, COLS), BF16),
            pltpu.VMEM((8, TOK, FEAT), BF16),
            pltpu.VMEM((TOK, FEAT), BF16),
            pltpu.VMEM((TOK, COLS), F32),
            pltpu.VMEM((TOK, FEAT), BF16),
            pltpu.VMEM((2, TOK, HD), BF16),
            pltpu.VMEM((TOK, COLS), BF16),
            pltpu.VMEM((2, COLS, TOK), BF16),
            pltpu.VMEM((2, TOK, HD), F32),
            pltpu.VMEM((TOK, HD), BF16),
            pltpu.VMEM((TOK, HD), BF16),
            pltpu.VMEM((16, TOK, FEAT), BF16),
            pltpu.VMEM((8, TOK, FEAT), BF16),
            pltpu.VMEM((8, HT, FEAT), BF16),
            pltpu.VMEM((2, TOK, FEAT), BF16),
            pltpu.VMEM((2, HT, FEAT), BF16),
            pltpu.VMEM((8, COLS, FEAT), BF16),
            pltpu.VMEM((4, COLS, FEAT), BF16),
            pltpu.VMEM((4, HG, FEAT), BF16),
            pltpu.VMEM((COLS, FEAT), BF16),
            pltpu.SemaphoreType.DMA((4,)),
            pltpu.SemaphoreType.DMA((N_SEMS,)),
            pltpu.SemaphoreType.DMA((N_SEMS,)),
        ],
        compiler_params=pltpu.CompilerParams(
            collective_id=0, has_side_effects=True, vmem_limit_bytes=60 * 2**20
        ),
        name="attention_backward",
    )(tokens_in, out_grad, q_weight, kv_weight, jnp.asarray(cosine), jnp.asarray(sine))


def solution(mesh):
    spec = P("dp", "tensor")
    return jax.shard_map(
        body, mesh=mesh, in_specs=(spec,) * 4, out_specs=(spec,) * 3, check_vma=False
    )
```

time: 497 us -> 161 us (0.32)
  waiting for transfers between devices: 410 us -> 0 us
  Pallas kernels: 0 us -> 155 us
  matrix products: 50.2 us -> 0 us
  between operations: 13.9 us -> 0.65 us
  other arithmetic: 9.86 us -> 0 us
  local copies, waits for them, and re-layouts: 10.1 us -> 3.51 us
    reduce_scatter x2 -> x0, waiting for transfers between devices: 221 us -> none  [the longest x1 111 us: body(): lax.psum_scatter(lax.dot_general(x_full, grads, (((0,), (0,)), ((), ())),...]
    pallas_call x0 -> x1, Pallas kernels: none -> 155 us  [body(): pl.pallas_call(kernel, out_shape=(jax.ShapeDtypeStruct((TOK, FEAT), BF16)...]
    all_gather x3 -> x0, waiting for transfers between devices: 128 us -> none  [the longest x1 47.3 us: body(): x_full = lax.all_gather(tokens_in, 'tensor', axis=1, tiled=True)]
    ppermute x2 -> x0, waiting for transfers between devices: 59.2 us -> none  [swapped(): return lax.ppermute(value, axis, pairs)]
    dot_general x9 -> x0, matrix products: 46.7 us -> none  [the longest x1 11.2 us: body(): lax.dot_general(x_full, grads, (((0,), (0,)), ((), ())), preferred_elemen...]
  transfers between devices with their start and end apart: 7 -> 0, of which waited for: 7 -> 0; matrix products, arithmetic and copies ran while one was open for 6% -> 0% of each run, Pallas kernels for 0% -> 0%
where the time goes in v1:
time: 161 us; the launch traced here: 159 us
  Pallas kernels  155 us (96%)
  local copies, waits for them, and re-layouts  3.51 us (2%)
    pallas_call x1, Pallas kernels, body(): pl.pallas_call(kernel, out_shape=(jax.ShapeDtypeStruct((TOK, FEAT), BF16)...  155 us
    unnamed x7, local copies, waits for them, and re-layouts  3.51 us

profile of v1, /device:TPU:1, one launch (start us, length us, event | category | flops | bytes accessed | tf_op | source)
XLA Modules:
  0.0 159.3 jit_solution(11419157054184308086)
XLA Ops:
  0.6 155.1 %attention_backward.1 = (bf16[384,512]{1,0:T(8,128)(2,1)}, bf16[512,512]{1,0:T(8,128)(2,1)}, bf16[512,128]{1,0:T(8,128)(2,1)}) custom-call(bf16[384,512]{1,0:T(8,128)(2,1)} %x_in.1, bf16[384,512]{1,0:T(8,128)(2,1)} %og_in.1, bf16[512,512]{1,0:T(8,128)(2,1)} %wq_in.1, bf16[512,128]{1,0:T(8,128)(2,1)} %wkv_in.1, f32[384,128]{1,0:T(8,128)} %constant.4.clone.cos_ref, ...), custom_call_target="tpu_custom_call" | custom-call | tf_op jit(solution)/shard_map/attention_backward/pallas_call | solution.py:430
  155.7 0.0 copy-start
  155.8 1.8 %copy.12 = bf16[384,512]{1,0:T(8,128)(2,1)} copy(bf16[384,512]{1,0:T(8,128)(2,1)} %get-tuple-element.6) | data formatting | bytes 786432
  157.6 0.0 copy-done
  157.6 0.0 copy-start.1
  157.6 0.8 copy.13
  158.4 0.2 copy-done.1
  158.6 0.7 copy.14
Async XLA Ops:
  155.7 1.8 %copy-start = (bf16[512,512]{1,0:T(8,128)(2,1)S(1)}, bf16[512,512]{1,0:T(8,128)(2,1)}, u32[]{:S(2)}) copy-start(bf16[512,512]{1,0:T(8,128)(2,1)} %get-tuple-element.7) | copy-start | bytes 1572868
  157.6 1.0 copy-start.1

commit v2 on v1

--- a/solution.py
+++ b/solution.py
@@ -12,6 +12,7 @@
 TOK, FEAT, HD, HEADS, COLS = 384, 512, 128, 4, 640
 HT, HW, HG = TOK // 2, FEAT // 2, COLS // 2
 N_SEMS = 192
+LOG2E = float(np.log2(np.e))
 
 
 def rope_tables(length, size):
@@ -41,8 +42,9 @@
 
 
 def kernel(
-    x_in, og_in, wq_in, wkv_in, cos_ref, sin_ref,
+    x_in, og_in, wq_in, wkv_in, cos_in, sin_in,
     dx_out, qg_out, kvg_out,
+    cos_ref, sin_ref, dx_st, qg_st, kvg_st,
     xbuf, wbuf, xsib, og, acc, qbuf, kv, gbuf, gt, part, part_low, part_in,
     dxs, ry_full, ry_half, rz_full, rz_half,
     dws, rx_full, rx_half, rzl,
@@ -96,18 +98,20 @@
         return wbuf.at[block, pl.ds(h * HW, HW)]
 
     own_x, own_w = tn, dp
+    barrier = pltpu.get_barrier_semaphore()
+    neighbours = (sib, zlp, xp, xm, yp, ym, zp, zm)
+    for to in neighbours:
+        pl.semaphore_signal(barrier, inc=1, device_id=to, device_id_type=MESH)
     loads = [
         pltpu.make_async_copy(x_in, xbuf.at[own_x], local_sem.at[0]),
         pltpu.make_async_copy(wq_in, wbuf.at[own_w, :, pl.ds(0, FEAT)], local_sem.at[1]),
         pltpu.make_async_copy(wkv_in, wbuf.at[own_w, :, pl.ds(FEAT, HD)], local_sem.at[2]),
         pltpu.make_async_copy(og_in, og, local_sem.at[3]),
+        pltpu.make_async_copy(cos_in, cos_ref, local_sem.at[4]),
+        pltpu.make_async_copy(sin_in, sin_ref, local_sem.at[5]),
     ]
     for load in loads:
         load.start()
-    barrier = pltpu.get_barrier_semaphore()
-    neighbours = (sib, zlp, xp, xm, yp, ym, zp, zm)
-    for to in neighbours:
-        pl.semaphore_signal(barrier, inc=1, device_id=to, device_id_type=MESH)
     pl.semaphore_wait(barrier, len(neighbours))
 
     def send_x(name, block, h, to):
@@ -176,6 +180,36 @@
         send_w(("xp", 1), block, h, xp)
         send_w(("xm", 1), block, h, xm)
         send_w("szl", block, h, sib)
+
+    acc[...] = jnp.zeros_like(acc)
+    part[...] = jnp.zeros_like(part)
+    for load in loads[3:]:
+        load.wait()
+    late = ((x + 2) % 4) * 2 + 1 - zl
+
+    def project(b, ready):
+        @pl.when(ready)
+        def _():
+            acc[...] += dot_nn(xbuf[b], wbuf[b])
+
+    def project_row(dh, dz):
+        first = ((zh + dh) % 4) * 4
+
+        def one(i, carry):
+            b = first + i
+            same = (b // 2) % 2 == zl
+            project(b, same if dz == 0 else jnp.logical_and(jnp.logical_not(same), b // 2 != late))
+            return carry
+
+        lax.fori_loop(0, 4, one, 0)
+
+    def rest_y(j):
+        recv_x(("yp", j), tb(j, 3), 1)
+        recv_x(("ym", j), tb(j, 1), 0)
+
+    def far_y(j):
+        recv_x(("ypr", j), tb(j, 2), 0)
+        recv_x(("ymr", j), tb(j, 2), 1)
 
     relay_y(0, 0)
     relay_y(0, 1)
@@ -201,39 +235,48 @@
     relay_y(3, 1)
     relay_y(1, 0)
     from_zl(1)
+    rest_y(0)
+    far_y(0)
+    for h in (0, 1):
+        recv_w("sib", wb(0, 0, 1), h)
+        recv_w(("sxp", 0), wb(3, 0, 1), h)
+        recv_w(("sxm", 0), wb(1, 0, 1), h)
+        recv_w(("sfar", 0), wb(2, 0, 1), h)
     recv_x("zpr", tb(2, 0), 0)
     spread_y(2, 0)
     recv_x("zmr", tb(2, 0), 1)
     spread_y(2, 1)
+    project_row(0, 0)
     relay_x(1, 0)
     relay_x(1, 1)
+    rest_y(3)
+    far_y(3)
+    project_row(3, 0)
     relay_y(2, 0)
     relay_y(2, 1)
+    rest_y(1)
+    far_y(1)
+    project_row(1, 0)
     rest_x(1)
+    for h in (0, 1):
+        recv_w("szl", wb(0, 1, 1), h)
+        recv_w(("sxp", 1), wb(3, 1, 1), h)
+        recv_w(("sxm", 1), wb(1, 1, 1), h)
+    project_row(0, 1)
     far_x(1)
-    for j in (0, 3, 1, 2):
-        recv_x(("yp", j), tb(j, 3), 1)
-        recv_x(("ym", j), tb(j, 1), 0)
-        recv_x(("ypr", j), tb(j, 2), 0)
-        recv_x(("ymr", j), tb(j, 2), 1)
+    project_row(3, 1)
+    project_row(1, 1)
+    rest_y(2)
+    far_y(2)
+    project_row(2, 0)
+    project_row(2, 1)
     for h in (0, 1):
-        recv_w("sib", wb(0, 0, 1), h)
-        recv_w("szl", wb(0, 1, 1), h)
-        for dz in (0, 1):
-            recv_w(("sxp", dz), wb(3, dz, 1), h)
-            recv_w(("sxm", dz), wb(1, dz, 1), h)
-            recv_w(("sfar", dz), wb(2, dz, 1), h)
-
-    for i in range(8):
-        send(("xsib", i), xbuf.at[2 * i + 1 - c], xsib.at[i], sib)
-
-    acc[...] = dot_nn(xbuf[0], wbuf[0])
-
-    def project(b, carry):
-        acc[...] += dot_nn(xbuf[b], wbuf[b])
-        return carry
-
-    lax.fori_loop(1, 16, project, 0)
+        recv_w(("sfar", 1), wb(2, 1, 1), h)
+    def last_two(cols):
+        b0, b1 = wb(2, 1, 0), wb(2, 1, 1)
+        acc[:, cols] += dot_nn(xbuf[b0], wbuf[b0, :, cols]) + dot_nn(xbuf[b1], wbuf[b1, :, cols])
+
+    last_two(slice(FEAT, COLS))
 
     def rot(u, rows=slice(None)):
         return u * cos_ref[rows, :] + pltpu.roll(u, HD // 2, 1) * sin_ref[rows, :]
@@ -244,49 +287,63 @@
     raw = acc[:, FEAT:COLS]
     kv[role] = jnp.where(is_key, rot(raw), raw).astype(BF16)
     send("kv", kv.at[role], kv.at[role], mate)
+
+    for i in range(8):
+        send(("xsib", i), xbuf.at[2 * i + 1 - c], xsib.at[i], sib)
+
+    last_two(slice(0, FEAT))
     for h in range(HEADS):
         qbuf[:, h * HD:(h + 1) * HD] = rot(acc[:, h * HD:(h + 1) * HD]).astype(BF16)
-    part[...] = jnp.zeros_like(part)
-    loads[3].wait()
     recv("kv", kv.at[1 - role])
 
     scale = HD ** -0.5
 
-    def head(h, carry):
-        cols = pl.ds(pl.multiple_of(h * HD, HD), HD)
-        for i in range(TOK // HD):
-            rows, n = slice(i * HD, (i + 1) * HD), (i + 1) * HD
+    for i in reversed(range(TOK // HD)):
+        rows, n = slice(i * HD, (i + 1) * HD), (i + 1) * HD
+
+        def head(h, carry, i=i, rows=rows, n=n):
+            cols = pl.ds(pl.multiple_of(h * HD, HD), HD)
             q, grad = qbuf[rows, cols], og[rows, cols]
             k, v = kv[0, :n], kv[1, :n]
-            scores = dot_nt(q, k) * scale
+            scores = dot_nt(q, k)
             q_pos = lax.broadcasted_iota(jnp.int32, (HD, n), 0) + i * HD
             k_pos = lax.broadcasted_iota(jnp.int32, (HD, n), 1)
             scores = jnp.where(k_pos <= q_pos, scores, -jnp.inf)
-            expo = jnp.exp(scores - jnp.max(scores, axis=-1, keepdims=True))
-            probs = expo / jnp.sum(expo, axis=-1, keepdims=True)
+            expo = jnp.exp2((scores - jnp.max(scores, axis=-1, keepdims=True)) * (scale * LOG2E))
+            probs = expo * (1.0 / jnp.sum(expo, axis=-1, keepdims=True))
             dprobs = dot_nt(grad, v)
             delta = jnp.sum(probs * dprobs, axis=-1, keepdims=True)
-            dscores = (probs * (dprobs - delta) * scale).astype(BF16)
+            dscores = (probs * ((dprobs - delta) * scale)).astype(BF16)
             dq = unrot(dot_nn(dscores, k), rows)
             gbuf[rows, cols] = dq.astype(BF16)
             gt[0, cols, rows] = dq.T.astype(BF16)
             part[0, :n] += dot_tn(dscores, q)
             part[1, :n] += dot_tn(probs.astype(BF16), grad)
-        return carry
-
-    lax.fori_loop(0, HEADS, head, 0)
-
-    part_low[...] = part[1 - role].astype(BF16)
-    send("part", part_low, part_in, mate)
+            return carry
+
+        lax.fori_loop(0, HEADS, head, 0, unroll=2 if i == 2 else 4)
+        part_low[rows, :] = part[1 - role, rows, :].astype(BF16)
+        send(("part", i), part_low.at[pl.ds(i * HD, HD)], part_in.at[pl.ds(i * HD, HD)], mate)
+
     send("gt_q", gt.at[0, pl.ds(0, FEAT)], gt.at[1, pl.ds(0, FEAT)], sib)
-    recv("part", part_in)
-    total = part[role] + part_in[...].astype(F32)
-    total = jnp.where(is_key, unrot(total), total)
-    gbuf[:, FEAT:COLS] = total.astype(BF16)
-    gt[0, FEAT:COLS, :] = total.T.astype(BF16)
+
+    first = tb(2, 2)
+    first_q = dot_nt(gbuf[:, :FEAT], wbuf[first, :, :FEAT])
+    for i in reversed(range(TOK // HD)):
+        rows = slice(i * HD, (i + 1) * HD)
+        recv(("part", i), part_in.at[pl.ds(i * HD, HD)])
+        total = part[role, rows, :] + part_in[rows, :].astype(F32)
+        total = jnp.where(is_key, unrot(total, rows), total)
+        gbuf[rows, FEAT:COLS] = total.astype(BF16)
+        gt[0, FEAT:COLS, rows] = total.T.astype(BF16)
     send("gt_kv", gt.at[0, pl.ds(FEAT, HD)], gt.at[1, pl.ds(FEAT, HD)], sib)
-    for i in range(8):
-        recv(("xsib", i), xsib.at[i])
+
+    stores = []
+
+    def store(src, dst):
+        copy = pltpu.make_async_copy(src, dst, local_sem.at[len(loads) + len(stores)])
+        copy.start()
+        stores.append(copy)
 
     def dx_half(j, dy, h):
         return dot_nt(gbuf[h * HT:(h + 1) * HT, :], wbuf[tb(j, dy)])
@@ -318,26 +375,28 @@
         dws[i, h * HG:(h + 1) * HG, :] = value.astype(BF16)
         send(name, gslot(dws, i, h), dst, to)
 
-    def s1(j):
-        put_dx(("s1", j, 0), j, 2, 0, dx_half(j, 2, 0), ry_half.at[j * 2], yp)
-        put_dx(("s1", j, 1), j, 2, 1, dx_half(j, 2, 1), ry_half.at[j * 2 + 1], ym)
-
-    def s2n(j):
-        put_dx(("s2", j, 0, 1), j, 1, 1, dx_half(j, 1, 1), tslot(ry_full, j * 2, 1), yp)
-        put_dx(("s2", j, 1, 0), j, 3, 0, dx_half(j, 3, 0), tslot(ry_full, j * 2 + 1, 0), ym)
-
-    def s2d(j):
-        mine = dx_half(j, 1, 0)
-        recv(("s1", j, 0), ry_half.at[j * 2])
-        put_dx(("s2", j, 0, 0), j, 1, 0, mine + ry_half[j * 2].astype(F32), tslot(ry_full, j * 2, 0), yp)
-        mine = dx_half(j, 3, 1)
-        recv(("s1", j, 1), ry_half.at[j * 2 + 1])
+    def s1(j0, j1, value0=None, value1=None):
+        value0 = dx_half(j0, 2, 0) if value0 is None else value0
+        put_dx(("s1", 0, j0), j0, 2, 0, value0, ry_half.at[j0 * 2], yp)
+        value1 = dx_half(j1, 2, 1) if value1 is None else value1
+        put_dx(("s1", 1, j1), j1, 2, 1, value1, ry_half.at[j1 * 2 + 1], ym)
+
+    def s2n(j0, j1):
+        put_dx(("s2", j1, 0, 1), j1, 1, 1, dx_half(j1, 1, 1), tslot(ry_full, j1 * 2, 1), yp)
+        put_dx(("s2", j0, 1, 0), j0, 3, 0, dx_half(j0, 3, 0), tslot(ry_full, j0 * 2 + 1, 0), ym)
+
+    def s2d(j0, j1):
+        mine = dx_half(j0, 1, 0)
+        recv(("s1", 0, j0), ry_half.at[j0 * 2])
+        put_dx(("s2", j0, 0, 0), j0, 1, 0, mine + ry_half[j0 * 2].astype(F32), tslot(ry_full, j0 * 2, 0), yp)
+        mine = dx_half(j1, 3, 1)
+        recv(("s1", 1, j1), ry_half.at[j1 * 2 + 1])
         put_dx(
-            ("s2", j, 1, 1), j, 3, 1, mine + ry_half[j * 2 + 1].astype(F32), tslot(ry_full, j * 2 + 1, 1), ym
+            ("s2", j1, 1, 1), j1, 3, 1, mine + ry_half[j1 * 2 + 1].astype(F32), tslot(ry_full, j1 * 2 + 1, 1), ym
         )
 
-    def s3(j):
-        for h in ((1, 0) if j == 1 else (0, 1)):
+    def s3(j0, j1):
+        for h, j in ((0, j0), (1, j1)):
             mine = dx_half(j, 0, h)
             recv(("s2", j, 0, h), tslot(ry_full, j * 2, h))
             recv(("s2", j, 1, h), tslot(ry_full, j * 2 + 1, h))
@@ -348,7 +407,8 @@
                 recv(("z2", 0, h), tslot(rz_full, 0, h))
                 recv(("z2", 1, h), tslot(rz_full, 1, h))
                 mine = mine + load_t(rz_full, 0, h) + load_t(rz_full, 1, h)
-                dx_out[h * HT:(h + 1) * HT, :] = mine.astype(BF16)
+                dx_st[h * HT:(h + 1) * HT, :] = mine.astype(BF16)
+                store(dx_st.at[pl.ds(h * HT, HT)], dx_out.at[pl.ds(h * HT, HT)])
             else:
                 side = 0 if j == 1 else 1
                 if h == side:
@@ -386,57 +446,92 @@
                 recv(("t3", h), rzl.at[pl.ds(h * HG, HG)])
                 mine = (mine + rzl[h * HG:(h + 1) * HG, :].astype(F32)).T.astype(BF16)
                 if h == 0:
-                    qg_out[:, :HG] = mine
+                    qg_st[:, :HG] = mine
+                    store(qg_st.at[:, pl.ds(0, HW)], qg_out.at[:, pl.ds(0, HW)])
                 else:
-                    qg_out[:, HG:] = mine[:, :FEAT - HG]
-                    kvg_out[...] = mine[:, FEAT - HG:]
-
-    s1(2)
+                    qg_st[:, HG:] = mine[:, :FEAT - HG]
+                    store(qg_st.at[:, pl.ds(HW, HW)], qg_out.at[:, pl.ds(HW, HW)])
+                    kvg_st[...] = mine[:, FEAT - HG:]
+                    store(kvg_st, kvg_out)
+
+    first_kv = dot_nt(gbuf[:, FEAT:COLS], wbuf[first, :, FEAT:COLS])
+    s1(2, 2, first_q[:HT] + first_kv[:HT], first_q[HT:] + first_kv[HT:])
+    for i in range(8):
+        recv(("xsib", i), xsib.at[i])
     recv("gt_q", gt.at[1, pl.ds(0, FEAT)])
     recv("gt_kv", gt.at[1, pl.ds(FEAT, HD)])
     t1(1)
-    s2n(2)
-    s1(1)
+    s2n(2, 2)
     t2n(1)
-    s2d(2)
-    s2n(1)
+    s1(3, 1)
+    s2d(2, 2)
+    s2n(3, 1)
+    t2d(1)
     t1(0)
-    s1(3)
-    s3(2)
-    s2d(1)
-    t2d(1)
-    s2n(3)
-    s1(0)
+    s1(1, 3)
+    s2d(3, 1)
+    s3(2, 2)
+    s2n(1, 3)
     t2n(0)
-    s3(1)
-    s2d(3)
     t3(1)
-    s2n(0)
+    s1(0, 0)
+    s2d(1, 3)
     t2d(0)
-    s3(3)
-    s2d(0)
+    s3(3, 1)
+    s2n(0, 0)
+    s2d(0, 0)
+    s3(1, 3)
     t3(0)
-    s3(0)
-
+    s3(0, 0)
+
+    for copy in stores:
+        copy.wait()
     for copy in pending:
         copy.wait_send()
     assert len(names) <= N_SEMS
 
 
+def hand_on(*refs):
+    n = len(refs) // 3
+    sources, targets, held = refs[:n], refs[n:2 * n], refs[2 * n:3 * n]
+    sem_in, sem_out = refs[3 * n:]
+    steps = []
+    for i in range(n):
+        size = held[i].shape[0] // 2
+        for h in (0, 1):
+            k, rows = 2 * i + h, pl.ds(h * size, size)
+            steps.append((
+                pltpu.make_async_copy(sources[i].at[rows], held[i].at[rows], sem_in.at[k]),
+                pltpu.make_async_copy(held[i].at[rows], targets[i].at[rows], sem_out.at[k]),
+            ))
+    for into, _ in steps:
+        into.start()
+    for into, out in steps:
+        into.wait()
+        out.start()
+    for _, out in steps:
+        out.wait()
+
+
 def body(tokens_in, out_grad, q_weight, kv_weight):
     cosine, sine = rope_tables(TOK, HD)
-    vmem = pl.BlockSpec(memory_space=pltpu.VMEM)
     anywhere = pl.BlockSpec(memory_space=pl.ANY)
-    return pl.pallas_call(
+    outs = (
+        jax.ShapeDtypeStruct((TOK, FEAT), BF16),
+        jax.ShapeDtypeStruct((FEAT, FEAT), BF16),
+        jax.ShapeDtypeStruct((FEAT, HD), BF16),
+    )
+    results = pl.pallas_call(
         kernel,
-        out_shape=(
-            jax.ShapeDtypeStruct((TOK, FEAT), BF16),
-            jax.ShapeDtypeStruct((FEAT, FEAT), BF16),
-            jax.ShapeDtypeStruct((FEAT, HD), BF16),
-        ),
-        in_specs=[anywhere] * 4 + [vmem] * 2,
-        out_specs=(vmem, vmem, vmem),
+        out_shape=outs,
+        in_specs=[anywhere] * 6,
+        out_specs=(anywhere,) * 3,
         scratch_shapes=[
+            pltpu.VMEM((TOK, HD), F32),
+            pltpu.VMEM((TOK, HD), F32),
+            pltpu.VMEM((TOK, FEAT), BF16),
+            pltpu.VMEM((FEAT, FEAT), BF16),
+            pltpu.VMEM((FEAT, HD), BF16),
             pltpu.VMEM((16, TOK, FEAT), BF16),
             pltpu.VMEM((16, FEAT, COLS), BF16),
             pltpu.VMEM((8, TOK, FEAT), BF16),
@@ -458,7 +553,7 @@
             pltpu.VMEM((4, COLS, FEAT), BF16),
             pltpu.VMEM((4, HG, FEAT), BF16),
             pltpu.VMEM((COLS, FEAT), BF16),
-            pltpu.SemaphoreType.DMA((4,)),
+            pltpu.SemaphoreType.DMA((12,)),
             pltpu.SemaphoreType.DMA((N_SEMS,)),
             pltpu.SemaphoreType.DMA((N_SEMS,)),
         ],
@@ -467,6 +562,14 @@
         ),
         name="attention_backward",
     )(tokens_in, out_grad, q_weight, kv_weight, jnp.asarray(cosine), jnp.asarray(sine))
+    return pl.pallas_call(
+        hand_on,
+        out_shape=outs,
+        in_specs=[anywhere] * 3,
+        out_specs=(anywhere,) * 3,
+        scratch_shapes=[pltpu.VMEM(o.shape, o.dtype) for o in outs] + [pltpu.SemaphoreType.DMA((6,))] * 2,
+        name="hand_on",
+    )(*results)
 
 
 def solution(mesh):

time: 161 us -> 148 us (0.919); the launches traced: 159 us -> 148 us
  Pallas kernels: 155 us -> 147 us
  local copies, waits for them, and re-layouts: 3.51 us -> 0 us
    pallas_call x1 -> x2, Pallas kernels: 155 us -> 147 us  [the longest x1 145 us: body(): pl.pallas_call(kernel, out_shape=outs, in_specs=[anywhere] * 6, out_specs...]
    unnamed x7 -> x0, local copies, waits for them, and re-layouts: 3.51 us -> none
where the time goes in v2:
time: 148 us
  Pallas kernels  147 us (99%)
    pallas_call x1, Pallas kernels, body(): pl.pallas_call(kernel, out_shape=outs, in_specs=[anywhere] * 6, out_specs...  145 us

profile of v2, /device:TPU:1, one launch (start us, length us, event | category | flops | bytes accessed | tf_op | source)
XLA Modules:
  0.0 148.1 jit_solution(15761687238719314227)
XLA Ops:
  0.6 145.3 %attention_backward.1 = (bf16[384,512]{1,0:T(8,128)(2,1)}, bf16[512,512]{1,0:T(8,128)(2,1)}, bf16[512,128]{1,0:T(8,128)(2,1)}) custom-call(bf16[384,512]{1,0:T(8,128)(2,1)} %x_in.1, bf16[384,512]{1,0:T(8,128)(2,1)} %og_in.1, bf16[512,512]{1,0:T(8,128)(2,1)} %wq_in.1, bf16[512,128]{1,0:T(8,128)(2,1)} %wkv_in.1, f32[384,128]{1,0:T(8,128)} %constant.4.clone.cos_in, ...), custom_call_target="tpu_custom_call" | custom-call | tf_op jit(solution)/shard_map/attention_backward/pallas_call | solution.py:524
  145.9 2.1 %hand_on.1 = (bf16[384,512]{1,0:T(8,128)(2,1)}, bf16[512,512]{1,0:T(8,128)(2,1)}, bf16[512,128]{1,0:T(8,128)(2,1)}) custom-call(bf16[384,512]{1,0:T(8,128)(2,1)} %get-tuple-element.6.refs_0_, bf16[512,512]{1,0:T(8,128)(2,1)} %get-tuple-element.7.refs_1_, bf16[512,128]{1,0:T(8,128)(2,1)} %get-tuple-element.8.refs_2_), custom_call_target="tpu_custom_call" | custom-call | tf_op jit(solution)/shard_map/hand_on/pallas_call | solution.py:565

commit v3 on v2

--- a/solution.py
+++ b/solution.py
@@ -10,8 +10,11 @@
 MESH = pl.DeviceIdType.MESH
 F32, BF16 = jnp.float32, jnp.bfloat16
 TOK, FEAT, HD, HEADS, COLS = 384, 512, 128, 4, 640
-HT, HW, HG = TOK // 2, FEAT // 2, COLS // 2
-N_SEMS = 192
+HT, HW = TOK // 2, FEAT // 2
+GC, GH = COLS // 2, COLS // 4
+CHUNKS = ((0, HD), (2 * HD, HD // 2))
+N_SEMS = 162
+N_SEND = 56
 LOG2E = float(np.log2(np.e))
 
 
@@ -44,7 +47,7 @@
 def kernel(
     x_in, og_in, wq_in, wkv_in, cos_in, sin_in,
     dx_out, qg_out, kvg_out,
-    cos_ref, sin_ref, dx_st, qg_st, kvg_st,
+    cos_ref, sin_ref, dx_st, qg_st, kvg_st, t_st,
     xbuf, wbuf, xsib, og, acc, qbuf, kv, gbuf, gt, part, part_low, part_in,
     dxs, ry_full, ry_half, rz_full, rz_half,
     dws, rx_full, rx_half, rzl,
@@ -76,9 +79,11 @@
         return names.setdefault(name, len(names))
 
     def send(name, src, dst, to):
-        k = sem(name)
+        k, n = sem(name), len(pending)
+        if n >= N_SEND:
+            pending[n - N_SEND].wait_send()
         copy = pltpu.make_async_remote_copy(
-            src_ref=src, dst_ref=dst, send_sem=ss.at[k], recv_sem=rs.at[k],
+            src_ref=src, dst_ref=dst, send_sem=ss.at[n % N_SEND], recv_sem=rs.at[k],
             device_id=to, device_id_type=MESH,
         )
         copy.start()
@@ -87,7 +92,7 @@
     def recv(name, dst):
         k = sem(name)
         pltpu.make_async_remote_copy(
-            src_ref=dst, dst_ref=dst, send_sem=ss.at[k], recv_sem=rs.at[k],
+            src_ref=dst, dst_ref=dst, send_sem=ss.at[0], recv_sem=rs.at[k],
             device_id=sib, device_id_type=MESH,
         ).wait_recv()
 
@@ -296,7 +301,134 @@
         qbuf[:, h * HD:(h + 1) * HD] = rot(acc[:, h * HD:(h + 1) * HD]).astype(BF16)
     recv("kv", kv.at[1 - role])
 
+    stores = []
+
+    def store(src, dst):
+        copy = pltpu.make_async_copy(src, dst, local_sem.at[len(loads) + len(stores)])
+        copy.start()
+        stores.append(copy)
+
+    def t_rows(ch, h):
+        first, size = CHUNKS[ch]
+        return slice(first + h * size, first + (h + 1) * size)
+
+    def t_part(ch):
+        return slice(0, HD) if ch == 0 else slice(HD, HD + HD // 2)
+
+    def g_rows(ch, h):
+        return slice(ch * GC + h * GH, ch * GC + (h + 1) * GH)
+
+    def g_part(ch):
+        return slice(ch * GH, (ch + 1) * GH)
+
+    def at(ref, i, rows):
+        return ref.at[i, pl.ds(rows.start, rows.stop - rows.start)]
+
+    def value(ref, i, rows):
+        return ref[i, rows, :].astype(F32)
+
+    def dx_half(j, dy, ch, h):
+        return dot_nt(gbuf[t_rows(ch, h), :], wbuf[tb(j, dy)])
+
+    def dw_half(ddx, dz, ch, h):
+        b, rows = wb(ddx, dz, 0), g_rows(ch, h)
+        return dot_nn(gt[0, rows, :], xbuf[b]) + dot_nn(gt[1, rows, :], xsib[b // 2])
+
+    def put_dx(name, j, dy, ch, h, mine, dst, to):
+        i, rows = j * 4 + dy, t_rows(ch, h)
+        dxs[i, rows, :] = mine.astype(BF16)
+        send(name, at(dxs, i, rows), dst, to)
+
+    def put_dw(name, ddx, dz, ch, h, mine, dst, to):
+        i, rows = ddx * 2 + dz, g_rows(ch, h)
+        dws[i, rows, :] = mine.astype(BF16)
+        send(name, at(dws, i, rows), dst, to)
+
+    def s1(ch, j0, j1):
+        for h, j, to in ((0, j0, yp), (1, j1, ym)):
+            put_dx(("s1", h, j, ch), j, 2, ch, h, dx_half(j, 2, ch, h), at(ry_half, j * 2 + h, t_part(ch)), to)
+
+    def s2n(ch, j0, j1):
+        for h, j, dy, way, to in ((1, j1, 1, 0, yp), (0, j0, 3, 1, ym)):
+            dst = at(ry_full, j * 2 + way, t_rows(ch, h))
+            put_dx(("s2", j, way, h, ch), j, dy, ch, h, dx_half(j, dy, ch, h), dst, to)
+
+    def s2d(ch, j0, j1):
+        for h, j, dy, to in ((0, j0, 1, yp), (1, j1, 3, ym)):
+            mine = dx_half(j, dy, ch, h)
+            recv(("s1", h, j, ch), at(ry_half, j * 2 + h, t_part(ch)))
+            mine = mine + value(ry_half, j * 2 + h, t_part(ch))
+            put_dx(("s2", j, h, h, ch), j, dy, ch, h, mine, at(ry_full, j * 2 + h, t_rows(ch, h)), to)
+
+    def s3(ch, j0, j1):
+        for h, j in ((0, j0), (1, j1)):
+            rows = t_rows(ch, h)
+            mine = dx_half(j, 0, ch, h)
+            for way in (0, 1):
+                recv(("s2", j, way, h, ch), at(ry_full, j * 2 + way, rows))
+                mine = mine + value(ry_full, j * 2 + way, rows)
+            if j == 2:
+                put_dx(("z1", h, ch), j, 0, ch, h, mine, at(rz_half, h, t_part(ch)), zp if h == 0 else zm)
+            elif j == 0:
+                for way in (0, 1):
+                    recv(("z2", way, h, ch), at(rz_full, way, rows))
+                    mine = mine + value(rz_full, way, rows)
+                dx_st[rows, :] = mine.astype(BF16)
+                part_rows = pl.ds(rows.start, rows.stop - rows.start)
+                store(dx_st.at[part_rows], dx_out.at[part_rows])
+            else:
+                way = 0 if j == 1 else 1
+                if h == way:
+                    recv(("z1", h, ch), at(rz_half, h, t_part(ch)))
+                    mine = mine + value(rz_half, h, t_part(ch))
+                put_dx(("z2", way, h, ch), j, 0, ch, h, mine, at(rz_full, way, rows), zp if j == 1 else zm)
+
+    def t1(dz, ch):
+        for h, to in ((0, xp), (1, xm)):
+            put_dw(("t1", h, dz, ch), 2, dz, ch, h, dw_half(2, dz, ch, h), at(rx_half, dz * 2 + h, g_part(ch)), to)
+
+    def t2n(dz, ch):
+        for h, ddx, way, to in ((1, 1, 0, xp), (0, 3, 1, xm)):
+            dst = at(rx_full, dz * 2 + way, g_rows(ch, h))
+            put_dw(("t2", dz, way, h, ch), ddx, dz, ch, h, dw_half(ddx, dz, ch, h), dst, to)
+
+    def t2d(dz, ch):
+        for h, ddx, to in ((0, 1, xp), (1, 3, xm)):
+            mine = dw_half(ddx, dz, ch, h)
+            recv(("t1", h, dz, ch), at(rx_half, dz * 2 + h, g_part(ch)))
+            mine = mine + value(rx_half, dz * 2 + h, g_part(ch))
+            put_dw(("t2", dz, h, h, ch), ddx, dz, ch, h, mine, at(rx_full, dz * 2 + h, g_rows(ch, h)), to)
+
+    def t3(dz, ch):
+        for h in (0, 1):
+            rows = g_rows(ch, h)
+            mine = dw_half(0, dz, ch, h)
+            for way in (0, 1):
+                recv(("t2", dz, way, h, ch), at(rx_full, dz * 2 + way, rows))
+                mine = mine + value(rx_full, dz * 2 + way, rows)
+            if dz == 1:
+                put_dw(("t3", h, ch), 0, 1, ch, h, mine, at(rzl, 0, rows), zlp)
+            else:
+                recv(("t3", h, ch), at(rzl, 0, rows))
+                t_st[rows, :] = mine + value(rzl, 0, rows)
+                for k in range(rows.start // HD, rows.stop // HD):
+                    block = t_st[k * HD:(k + 1) * HD, :].T.astype(BF16)
+                    if k < HEADS:
+                        qg_st[:, k * HD:(k + 1) * HD] = block
+                        store(qg_st.at[:, pl.ds(k * HD, HD)], qg_out.at[:, pl.ds(k * HD, HD)])
+                    else:
+                        kvg_st[...] = block
+                        store(kvg_st, kvg_out)
+
     scale = HD ** -0.5
+
+    def finish_role(i):
+        rows = slice(i * HD, (i + 1) * HD)
+        recv(("part", i), part_in.at[pl.ds(i * HD, HD)])
+        total = part[role, rows, :] + part_in[rows, :].astype(F32)
+        total = jnp.where(is_key, unrot(total, rows), total)
+        gbuf[rows, FEAT:COLS] = total.astype(BF16)
+        gt[0, FEAT:COLS, rows] = total.T.astype(BF16)
 
     for i in reversed(range(TOK // HD)):
         rows, n = slice(i * HD, (i + 1) * HD), (i + 1) * HD
@@ -324,169 +456,69 @@
         lax.fori_loop(0, HEADS, head, 0, unroll=2 if i == 2 else 4)
         part_low[rows, :] = part[1 - role, rows, :].astype(BF16)
         send(("part", i), part_low.at[pl.ds(i * HD, HD)], part_in.at[pl.ds(i * HD, HD)], mate)
+        if i == 1:
+            finish_role(2)
+            s1(1, 2, 2)
+            s2n(1, 2, 2)
+            s1(1, 3, 1)
 
     send("gt_q", gt.at[0, pl.ds(0, FEAT)], gt.at[1, pl.ds(0, FEAT)], sib)
-
-    first = tb(2, 2)
-    first_q = dot_nt(gbuf[:, :FEAT], wbuf[first, :, :FEAT])
-    for i in reversed(range(TOK // HD)):
-        rows = slice(i * HD, (i + 1) * HD)
-        recv(("part", i), part_in.at[pl.ds(i * HD, HD)])
-        total = part[role, rows, :] + part_in[rows, :].astype(F32)
-        total = jnp.where(is_key, unrot(total, rows), total)
-        gbuf[rows, FEAT:COLS] = total.astype(BF16)
-        gt[0, FEAT:COLS, rows] = total.T.astype(BF16)
-    send("gt_kv", gt.at[0, pl.ds(FEAT, HD)], gt.at[1, pl.ds(FEAT, HD)], sib)
-
-    stores = []
-
-    def store(src, dst):
-        copy = pltpu.make_async_copy(src, dst, local_sem.at[len(loads) + len(stores)])
-        copy.start()
-        stores.append(copy)
-
-    def dx_half(j, dy, h):
-        return dot_nt(gbuf[h * HT:(h + 1) * HT, :], wbuf[tb(j, dy)])
-
-    def dw_half(ddx, dz, h):
-        b = wb(ddx, dz, 0)
-        rows = slice(h * HG, (h + 1) * HG)
-        return dot_nn(gt[0, rows, :], xbuf[b]) + dot_nn(gt[1, rows, :], xsib[b // 2])
-
-    def tslot(ref, i, h):
-        return ref.at[i, pl.ds(h * HT, HT)]
-
-    def gslot(ref, i, h):
-        return ref.at[i, pl.ds(h * HG, HG)]
-
-    def load_t(ref, i, h):
-        return ref[i, h * HT:(h + 1) * HT, :].astype(F32)
-
-    def load_g(ref, i, h):
-        return ref[i, h * HG:(h + 1) * HG, :].astype(F32)
-
-    def put_dx(name, j, dy, h, value, dst, to):
-        i = j * 4 + dy
-        dxs[i, h * HT:(h + 1) * HT, :] = value.astype(BF16)
-        send(name, tslot(dxs, i, h), dst, to)
-
-    def put_dw(name, ddx, dz, h, value, dst, to):
-        i = ddx * 2 + dz
-        dws[i, h * HG:(h + 1) * HG, :] = value.astype(BF16)
-        send(name, gslot(dws, i, h), dst, to)
-
-    def s1(j0, j1, value0=None, value1=None):
-        value0 = dx_half(j0, 2, 0) if value0 is None else value0
-        put_dx(("s1", 0, j0), j0, 2, 0, value0, ry_half.at[j0 * 2], yp)
-        value1 = dx_half(j1, 2, 1) if value1 is None else value1
-        put_dx(("s1", 1, j1), j1, 2, 1, value1, ry_half.at[j1 * 2 + 1], ym)
-
-    def s2n(j0, j1):
-        put_dx(("s2", j1, 0, 1), j1, 1, 1, dx_half(j1, 1, 1), tslot(ry_full, j1 * 2, 1), yp)
-        put_dx(("s2", j0, 1, 0), j0, 3, 0, dx_half(j0, 3, 0), tslot(ry_full, j0 * 2 + 1, 0), ym)
-
-    def s2d(j0, j1):
-        mine = dx_half(j0, 1, 0)
-        recv(("s1", 0, j0), ry_half.at[j0 * 2])
-        put_dx(("s2", j0, 0, 0), j0, 1, 0, mine + ry_half[j0 * 2].astype(F32), tslot(ry_full, j0 * 2, 0), yp)
-        mine = dx_half(j1, 3, 1)
-        recv(("s1", 1, j1), ry_half.at[j1 * 2 + 1])
-        put_dx(
-            ("s2", j1, 1, 1), j1, 3, 1, mine + ry_half[j1 * 2 + 1].astype(F32), tslot(ry_full, j1 * 2 + 1, 1), ym
-        )
-
-    def s3(j0, j1):
-        for h, j in ((0, j0), (1, j1)):
-            mine = dx_half(j, 0, h)
-            recv(("s2", j, 0, h), tslot(ry_full, j * 2, h))
-            recv(("s2", j, 1, h), tslot(ry_full, j * 2 + 1, h))
-            mine = mine + load_t(ry_full, j * 2, h) + load_t(ry_full, j * 2 + 1, h)
-            if j == 2:
-                put_dx(("z1", h), 2, 0, h, mine, rz_half.at[h], zp if h == 0 else zm)
-            elif j == 0:
-                recv(("z2", 0, h), tslot(rz_full, 0, h))
-                recv(("z2", 1, h), tslot(rz_full, 1, h))
-                mine = mine + load_t(rz_full, 0, h) + load_t(rz_full, 1, h)
-                dx_st[h * HT:(h + 1) * HT, :] = mine.astype(BF16)
-                store(dx_st.at[pl.ds(h * HT, HT)], dx_out.at[pl.ds(h * HT, HT)])
-            else:
-                side = 0 if j == 1 else 1
-                if h == side:
-                    recv(("z1", side), rz_half.at[side])
-                    mine = mine + rz_half[side].astype(F32)
-                put_dx(("z2", side, h), j, 0, h, mine, tslot(rz_full, side, h), zp if j == 1 else zm)
-
-    def t1(dz):
-        put_dw(("t1", dz, 0), 2, dz, 0, dw_half(2, dz, 0), rx_half.at[dz * 2], xp)
-        put_dw(("t1", dz, 1), 2, dz, 1, dw_half(2, dz, 1), rx_half.at[dz * 2 + 1], xm)
-
-    def t2n(dz):
-        put_dw(("t2", dz, 0, 1), 1, dz, 1, dw_half(1, dz, 1), gslot(rx_full, dz * 2, 1), xp)
-        put_dw(("t2", dz, 1, 0), 3, dz, 0, dw_half(3, dz, 0), gslot(rx_full, dz * 2 + 1, 0), xm)
-
-    def t2d(dz):
-        mine = dw_half(1, dz, 0)
-        recv(("t1", dz, 0), rx_half.at[dz * 2])
-        put_dw(("t2", dz, 0, 0), 1, dz, 0, mine + rx_half[dz * 2].astype(F32), gslot(rx_full, dz * 2, 0), xp)
-        mine = dw_half(3, dz, 1)
-        recv(("t1", dz, 1), rx_half.at[dz * 2 + 1])
-        put_dw(
-            ("t2", dz, 1, 1), 3, dz, 1, mine + rx_half[dz * 2 + 1].astype(F32), gslot(rx_full, dz * 2 + 1, 1), xm
-        )
-
-    def t3(dz):
-        for h in (0, 1):
-            mine = dw_half(0, dz, h)
-            recv(("t2", dz, 0, h), gslot(rx_full, dz * 2, h))
-            recv(("t2", dz, 1, h), gslot(rx_full, dz * 2 + 1, h))
-            mine = mine + load_g(rx_full, dz * 2, h) + load_g(rx_full, dz * 2 + 1, h)
-            if dz == 1:
-                put_dw(("t3", h), 0, 1, h, mine, rzl.at[pl.ds(h * HG, HG)], zlp)
-            else:
-                recv(("t3", h), rzl.at[pl.ds(h * HG, HG)])
-                mine = (mine + rzl[h * HG:(h + 1) * HG, :].astype(F32)).T.astype(BF16)
-                if h == 0:
-                    qg_st[:, :HG] = mine
-                    store(qg_st.at[:, pl.ds(0, HW)], qg_out.at[:, pl.ds(0, HW)])
-                else:
-                    qg_st[:, HG:] = mine[:, :FEAT - HG]
-                    store(qg_st.at[:, pl.ds(HW, HW)], qg_out.at[:, pl.ds(HW, HW)])
-                    kvg_st[...] = mine[:, FEAT - HG:]
-                    store(kvg_st, kvg_out)
-
-    first_kv = dot_nt(gbuf[:, FEAT:COLS], wbuf[first, :, FEAT:COLS])
-    s1(2, 2, first_q[:HT] + first_kv[:HT], first_q[HT:] + first_kv[HT:])
+    s2d(1, 2, 2)
     for i in range(8):
         recv(("xsib", i), xsib.at[i])
     recv("gt_q", gt.at[1, pl.ds(0, FEAT)])
+    t1(1, 0)
+    t2n(1, 0)
+    finish_role(1)
+    finish_role(0)
+    send("gt_kv", gt.at[0, pl.ds(FEAT, HD)], gt.at[1, pl.ds(FEAT, HD)], sib)
+    s1(0, 2, 2)
+    s2n(1, 3, 1)
+    s3(1, 2, 2)
+    t2d(1, 0)
+    s2n(0, 2, 2)
     recv("gt_kv", gt.at[1, pl.ds(FEAT, HD)])
-    t1(1)
-    s2n(2, 2)
-    t2n(1)
-    s1(3, 1)
-    s2d(2, 2)
-    s2n(3, 1)
-    t2d(1)
-    t1(0)
-    s1(1, 3)
-    s2d(3, 1)
-    s3(2, 2)
-    s2n(1, 3)
-    t2n(0)
-    t3(1)
-    s1(0, 0)
-    s2d(1, 3)
-    t2d(0)
-    s3(3, 1)
-    s2n(0, 0)
-    s2d(0, 0)
-    s3(1, 3)
-    t3(0)
-    s3(0, 0)
+    t1(1, 1)
+    s2d(1, 3, 1)
+    s1(1, 1, 3)
+    t2n(1, 1)
+    s2n(1, 1, 3)
+    s2d(0, 2, 2)
+    s1(0, 3, 1)
+    s3(1, 3, 1)
+    t3(1, 0)
+    t2d(1, 1)
+    t1(0, 0)
+    s2d(1, 1, 3)
+    s2n(0, 3, 1)
+    s3(0, 2, 2)
+    s2d(0, 3, 1)
+    t2n(0, 0)
+    s1(0, 1, 3)
+    s2n(0, 1, 3)
+    t2d(0, 0)
+    t1(0, 1)
+    s3(1, 1, 3)
+    s3(0, 3, 1)
+    t3(1, 1)
+    s2d(0, 1, 3)
+    t2n(0, 1)
+    s1(1, 0, 0)
+    s2n(1, 0, 0)
+    s1(0, 0, 0)
+    s2n(0, 0, 0)
+    t2d(0, 1)
+    s2d(1, 0, 0)
+    t3(0, 0)
+    s3(0, 1, 3)
+    s2d(0, 0, 0)
+    s3(1, 0, 0)
+    t3(0, 1)
+    s3(0, 0, 0)
 
     for copy in stores:
         copy.wait()
-    for copy in pending:
+    for copy in pending[-N_SEND:]:
         copy.wait_send()
     assert len(names) <= N_SEMS
 
@@ -532,6 +564,7 @@
             pltpu.VMEM((TOK, FEAT), BF16),
             pltpu.VMEM((FEAT, FEAT), BF16),
             pltpu.VMEM((FEAT, HD), BF16),
+            pltpu.VMEM((COLS, FEAT), F32),
             pltpu.VMEM((16, TOK, FEAT), BF16),
             pltpu.VMEM((16, FEAT, COLS), BF16),
             pltpu.VMEM((8, TOK, FEAT), BF16),
@@ -551,10 +584,10 @@
             pltpu.VMEM((2, HT, FEAT), BF16),
             pltpu.VMEM((8, COLS, FEAT), BF16),
             pltpu.VMEM((4, COLS, FEAT), BF16),
-            pltpu.VMEM((4, HG, FEAT), BF16),
-            pltpu.VMEM((COLS, FEAT), BF16),
-            pltpu.SemaphoreType.DMA((12,)),
-            pltpu.SemaphoreType.DMA((N_SEMS,)),
+            pltpu.VMEM((4, GC, FEAT), BF16),
+            pltpu.VMEM((1, COLS, FEAT), BF16),
+            pltpu.SemaphoreType.DMA((16,)),
+            pltpu.SemaphoreType.DMA((N_SEND,)),
             pltpu.SemaphoreType.DMA((N_SEMS,)),
         ],
         compiler_params=pltpu.CompilerParams(

time: 148 us -> 141 us (0.953)
  Pallas kernels: 147 us -> 140 us
    pallas_call x1, Pallas kernels: 145 us -> 138 us  [body(): pl.pallas_call(kernel, out_shape=outs, in_specs=[anywhere] * 6, out_specs...]
where the time goes in v3:
time: 141 us; the launch traced here: 140 us
  Pallas kernels  140 us (99%)
    pallas_call x1, Pallas kernels, body(): pl.pallas_call(kernel, out_shape=outs, in_specs=[anywhere] * 6, out_specs...  138 us

profile of v3, /device:TPU:1, one launch (start us, length us, event | category | flops | bytes accessed | tf_op | source)
XLA Modules:
  0.0 140.4 jit_solution(4938748637790509353)
XLA Ops:
  0.6 137.5 %attention_backward.1 = (bf16[384,512]{1,0:T(8,128)(2,1)}, bf16[512,512]{1,0:T(8,128)(2,1)}, bf16[512,128]{1,0:T(8,128)(2,1)}) custom-call(bf16[384,512]{1,0:T(8,128)(2,1)} %x_in.1, bf16[384,512]{1,0:T(8,128)(2,1)} %og_in.1, bf16[512,512]{1,0:T(8,128)(2,1)} %wq_in.1, bf16[512,128]{1,0:T(8,128)(2,1)} %wkv_in.1, f32[384,128]{1,0:T(8,128)} %constant.4.clone.cos_in, ...), custom_call_target="tpu_custom_call" | custom-call | tf_op jit(solution)/shard_map/attention_backward/pallas_call | solution.py:556
  138.2 2.1 %hand_on.1 = (bf16[384,512]{1,0:T(8,128)(2,1)}, bf16[512,512]{1,0:T(8,128)(2,1)}, bf16[512,128]{1,0:T(8,128)(2,1)}) custom-call(bf16[384,512]{1,0:T(8,128)(2,1)} %get-tuple-element.6.refs_0_, bf16[512,512]{1,0:T(8,128)(2,1)} %get-tuple-element.7.refs_1_, bf16[512,128]{1,0:T(8,128)(2,1)} %get-tuple-element.8.refs_2_), custom_call_target="tpu_custom_call" | custom-call | tf_op jit(solution)/shard_map/hand_on/pallas_call | solution.py:598

commit v4 on v3

--- a/solution.py
+++ b/solution.py
@@ -13,7 +13,9 @@
 HT, HW = TOK // 2, FEAT // 2
 GC, GH = COLS // 2, COLS // 4
 CHUNKS = ((0, HD), (2 * HD, HD // 2))
-N_SEMS = 162
+LAST = 32
+MOST = TOK - LAST
+N_SEMS = 166
 N_SEND = 56
 LOG2E = float(np.log2(np.e))
 
@@ -49,7 +51,7 @@
     dx_out, qg_out, kvg_out,
     cos_ref, sin_ref, dx_st, qg_st, kvg_st, t_st,
     xbuf, wbuf, xsib, og, acc, qbuf, kv, gbuf, gt, part, part_low, part_in,
-    dxs, ry_full, ry_half, rz_full, rz_half,
+    dxs, ry_full, ry_half, rz_full, rz_half, rq_full, rq_half,
     dws, rx_full, rx_half, rzl,
     local_sem, ss, rs,
 ):
@@ -192,18 +194,20 @@
         load.wait()
     late = ((x + 2) % 4) * 2 + 1 - zl
 
-    def project(b, ready):
+    both, q_cols, kv_cols = slice(0, COLS), slice(0, FEAT), slice(FEAT, COLS)
+
+    def project(b, ready, cols):
         @pl.when(ready)
         def _():
-            acc[...] += dot_nn(xbuf[b], wbuf[b])
-
-    def project_row(dh, dz):
+            acc[:, cols] += dot_nn(xbuf[b], wbuf[b, :, cols])
+
+    def project_row(dh, dz, cols=both):
         first = ((zh + dh) % 4) * 4
 
         def one(i, carry):
             b = first + i
             same = (b // 2) % 2 == zl
-            project(b, same if dz == 0 else jnp.logical_and(jnp.logical_not(same), b // 2 != late))
+            project(b, same if dz == 0 else jnp.logical_and(jnp.logical_not(same), b // 2 != late), cols)
             return carry
 
         lax.fori_loop(0, 4, one, 0)
@@ -273,15 +277,15 @@
     project_row(1, 1)
     rest_y(2)
     far_y(2)
-    project_row(2, 0)
-    project_row(2, 1)
+    project_row(2, 0, kv_cols)
+    project_row(2, 1, kv_cols)
     for h in (0, 1):
         recv_w(("sfar", 1), wb(2, 1, 1), h)
     def last_two(cols):
         b0, b1 = wb(2, 1, 0), wb(2, 1, 1)
         acc[:, cols] += dot_nn(xbuf[b0], wbuf[b0, :, cols]) + dot_nn(xbuf[b1], wbuf[b1, :, cols])
 
-    last_two(slice(FEAT, COLS))
+    last_two(kv_cols)
 
     def rot(u, rows=slice(None)):
         return u * cos_ref[rows, :] + pltpu.roll(u, HD // 2, 1) * sin_ref[rows, :]
@@ -296,7 +300,9 @@
     for i in range(8):
         send(("xsib", i), xbuf.at[2 * i + 1 - c], xsib.at[i], sib)
 
-    last_two(slice(0, FEAT))
+    project_row(2, 0, q_cols)
+    project_row(2, 1, q_cols)
+    last_two(q_cols)
     for h in range(HEADS):
         qbuf[:, h * HD:(h + 1) * HD] = rot(acc[:, h * HD:(h + 1) * HD]).astype(BF16)
     recv("kv", kv.at[1 - role])
@@ -308,12 +314,17 @@
         copy.start()
         stores.append(copy)
 
-    def t_rows(ch, h):
+    def t_rows(ch, h, j):
         first, size = CHUNKS[ch]
+        if ch == 1 and j != 0:
+            size -= LAST // 2
         return slice(first + h * size, first + (h + 1) * size)
 
-    def t_part(ch):
-        return slice(0, HD) if ch == 0 else slice(HD, HD + HD // 2)
+    def t_part(ch, j):
+        first, (_, size) = (0, HD)[ch], CHUNKS[ch]
+        if ch == 1 and j != 0:
+            size -= LAST // 2
+        return slice(first, first + size)
 
     def g_rows(ch, h):
         return slice(ch * GC + h * GH, ch * GC + (h + 1) * GH)
@@ -328,14 +339,49 @@
         return ref[i, rows, :].astype(F32)
 
     def dx_half(j, dy, ch, h):
-        return dot_nt(gbuf[t_rows(ch, h), :], wbuf[tb(j, dy)])
+        mine = dot_nt(gbuf[t_rows(ch, h, j), :], wbuf[tb(j, dy)])
+        if (j, ch, h) == (0, 1, 1):
+            over_z = rq_full[0, dy].astype(F32) + rq_full[1, dy].astype(F32)
+            mine = jnp.concatenate([mine[:-LAST], mine[-LAST:] + over_z], axis=0)
+        return mine
+
+    def last_rows(j):
+        return [dot_nt(gbuf[MOST:, :], wbuf[tb(j, dy)]) for dy in range(4)]
+
+    def put_last(name, j, values, part, dst, to):
+        for dy in range(4):
+            dxs[j * 4 + dy, MOST:, :] = values[dy].astype(BF16)
+        send(name, dxs.at[pl.ds(j * 4, 4), pl.ds(MOST + part.start, part.stop - part.start)], dst, to)
+
+    def q1():
+        values, half = last_rows(2), LAST // 2
+        put_last(("q1", 0), 2, values, slice(0, half), rq_half.at[0], zp)
+        send(("q1", 1), dxs.at[pl.ds(8, 4), pl.ds(MOST + half, half)], rq_half.at[1], zm)
+
+    def q2():
+        half = LAST // 2
+        for way, j, to in ((0, 1, zp), (1, 3, zm)):
+            values = last_rows(j)
+            recv(("q1", way), rq_half.at[way])
+            for dy in range(4):
+                first, second = values[dy][:half], values[dy][half:]
+                if way == 0:
+                    first = first + rq_half[0, dy].astype(F32)
+                else:
+                    second = second + rq_half[1, dy].astype(F32)
+                values[dy] = jnp.concatenate([first, second], axis=0)
+            put_last(("q2", way), j, values, slice(0, LAST), rq_full.at[way], to)
+
+    def q3():
+        for way in (0, 1):
+            recv(("q2", way), rq_full.at[way])
 
     def dw_half(ddx, dz, ch, h):
         b, rows = wb(ddx, dz, 0), g_rows(ch, h)
         return dot_nn(gt[0, rows, :], xbuf[b]) + dot_nn(gt[1, rows, :], xsib[b // 2])
 
     def put_dx(name, j, dy, ch, h, mine, dst, to):
-        i, rows = j * 4 + dy, t_rows(ch, h)
+        i, rows = j * 4 + dy, t_rows(ch, h, j)
         dxs[i, rows, :] = mine.astype(BF16)
         send(name, at(dxs, i, rows), dst, to)
 
@@ -346,41 +392,46 @@
 
     def s1(ch, j0, j1):
         for h, j, to in ((0, j0, yp), (1, j1, ym)):
-            put_dx(("s1", h, j, ch), j, 2, ch, h, dx_half(j, 2, ch, h), at(ry_half, j * 2 + h, t_part(ch)), to)
+            put_dx(("s1", h, j, ch), j, 2, ch, h, dx_half(j, 2, ch, h), at(ry_half, j * 2 + h, t_part(ch, j)), to)
 
     def s2n(ch, j0, j1):
         for h, j, dy, way, to in ((1, j1, 1, 0, yp), (0, j0, 3, 1, ym)):
-            dst = at(ry_full, j * 2 + way, t_rows(ch, h))
+            dst = at(ry_full, j * 2 + way, t_rows(ch, h, j))
             put_dx(("s2", j, way, h, ch), j, dy, ch, h, dx_half(j, dy, ch, h), dst, to)
 
     def s2d(ch, j0, j1):
         for h, j, dy, to in ((0, j0, 1, yp), (1, j1, 3, ym)):
             mine = dx_half(j, dy, ch, h)
-            recv(("s1", h, j, ch), at(ry_half, j * 2 + h, t_part(ch)))
-            mine = mine + value(ry_half, j * 2 + h, t_part(ch))
-            put_dx(("s2", j, h, h, ch), j, dy, ch, h, mine, at(ry_full, j * 2 + h, t_rows(ch, h)), to)
+            recv(("s1", h, j, ch), at(ry_half, j * 2 + h, t_part(ch, j)))
+            mine = mine + value(ry_half, j * 2 + h, t_part(ch, j))
+            put_dx(("s2", j, h, h, ch), j, dy, ch, h, mine, at(ry_full, j * 2 + h, t_rows(ch, h, j)), to)
 
     def s3(ch, j0, j1):
         for h, j in ((0, j0), (1, j1)):
-            rows = t_rows(ch, h)
+            rows = t_rows(ch, h, j)
             mine = dx_half(j, 0, ch, h)
             for way in (0, 1):
                 recv(("s2", j, way, h, ch), at(ry_full, j * 2 + way, rows))
                 mine = mine + value(ry_full, j * 2 + way, rows)
             if j == 2:
-                put_dx(("z1", h, ch), j, 0, ch, h, mine, at(rz_half, h, t_part(ch)), zp if h == 0 else zm)
+                put_dx(("z1", h, ch), j, 0, ch, h, mine, at(rz_half, h, t_part(ch, j)), zp if h == 0 else zm)
             elif j == 0:
                 for way in (0, 1):
-                    recv(("z2", way, h, ch), at(rz_full, way, rows))
-                    mine = mine + value(rz_full, way, rows)
+                    for part in ((h,) if ch == 0 else (0, 1) if h == 0 else ()):
+                        recv(("z2", way, part, ch), at(rz_full, way, t_rows(ch, part, 1)))
+                    if ch == 1 and h == 1:
+                        over_z = value(rz_full, way, slice(rows.start, MOST))
+                        mine = jnp.concatenate([mine[:-LAST] + over_z, mine[-LAST:]], axis=0)
+                    else:
+                        mine = mine + value(rz_full, way, rows)
                 dx_st[rows, :] = mine.astype(BF16)
                 part_rows = pl.ds(rows.start, rows.stop - rows.start)
                 store(dx_st.at[part_rows], dx_out.at[part_rows])
             else:
                 way = 0 if j == 1 else 1
                 if h == way:
-                    recv(("z1", h, ch), at(rz_half, h, t_part(ch)))
-                    mine = mine + value(rz_half, h, t_part(ch))
+                    recv(("z1", h, ch), at(rz_half, h, t_part(ch, j)))
+                    mine = mine + value(rz_half, h, t_part(ch, j))
                 put_dx(("z2", way, h, ch), j, 0, ch, h, mine, at(rz_full, way, rows), zp if j == 1 else zm)
 
     def t1(dz, ch):
@@ -463,6 +514,7 @@
             s1(1, 3, 1)
 
     send("gt_q", gt.at[0, pl.ds(0, FEAT)], gt.at[1, pl.ds(0, FEAT)], sib)
+    q1()
     s2d(1, 2, 2)
     for i in range(8):
         recv(("xsib", i), xsib.at[i])
@@ -473,6 +525,7 @@
     finish_role(0)
     send("gt_kv", gt.at[0, pl.ds(FEAT, HD)], gt.at[1, pl.ds(FEAT, HD)], sib)
     s1(0, 2, 2)
+    q2()
     s2n(1, 3, 1)
     s3(1, 2, 2)
     t2d(1, 0)
@@ -503,6 +556,7 @@
     t3(1, 1)
     s2d(0, 1, 3)
     t2n(0, 1)
+    q3()
     s1(1, 0, 0)
     s2n(1, 0, 0)
     s1(0, 0, 0)
@@ -582,6 +636,8 @@
             pltpu.VMEM((8, HT, FEAT), BF16),
             pltpu.VMEM((2, TOK, FEAT), BF16),
             pltpu.VMEM((2, HT, FEAT), BF16),
+            pltpu.VMEM((2, 4, LAST, FEAT), BF16),
+            pltpu.VMEM((2, 4, LAST // 2, FEAT), BF16),
             pltpu.VMEM((8, COLS, FEAT), BF16),
             pltpu.VMEM((4, COLS, FEAT), BF16),
             pltpu.VMEM((4, GC, FEAT), BF16),

time: 141 us -> 139 us (0.986)
  Pallas kernels: 140 us -> 137 us
    pallas_call x1, Pallas kernels: 138 us -> 135 us  [body(): pl.pallas_call(kernel, out_shape=outs, in_specs=[anywhere] * 6, out_specs...]
where the time goes in v4:
time: 139 us; the launch traced here: 138 us
  Pallas kernels  137 us (99%)
    pallas_call x1, Pallas kernels, body(): pl.pallas_call(kernel, out_shape=outs, in_specs=[anywhere] * 6, out_specs...  135 us

profile of v4, /device:TPU:1, one launch (start us, length us, event | category | flops | bytes accessed | tf_op | source)
XLA Modules:
  0.0 138.2 jit_solution(16083555107499845017)
XLA Ops:
  0.6 135.3 %attention_backward.1 = (bf16[384,512]{1,0:T(8,128)(2,1)}, bf16[512,512]{1,0:T(8,128)(2,1)}, bf16[512,128]{1,0:T(8,128)(2,1)}) custom-call(bf16[384,512]{1,0:T(8,128)(2,1)} %x_in.1, bf16[384,512]{1,0:T(8,128)(2,1)} %og_in.1, bf16[512,512]{1,0:T(8,128)(2,1)} %wq_in.1, bf16[512,128]{1,0:T(8,128)(2,1)} %wkv_in.1, f32[384,128]{1,0:T(8,128)} %constant.4.clone.cos_in, ...), custom_call_target="tpu_custom_call" | custom-call | tf_op jit(solution)/shard_map/attention_backward/pallas_call | solution.py:610
  135.9 2.1 %hand_on.1 = (bf16[384,512]{1,0:T(8,128)(2,1)}, bf16[512,512]{1,0:T(8,128)(2,1)}, bf16[512,128]{1,0:T(8,128)(2,1)}) custom-call(bf16[384,512]{1,0:T(8,128)(2,1)} %get-tuple-element.6.refs_0_, bf16[512,512]{1,0:T(8,128)(2,1)} %get-tuple-element.7.refs_1_, bf16[512,128]{1,0:T(8,128)(2,1)} %get-tuple-element.8.refs_2_), custom_call_target="tpu_custom_call" | custom-call | tf_op jit(solution)/shard_map/hand_on/pallas_call | solution.py:654

commit v5 on v4

--- a/solution.py
+++ b/solution.py
@@ -489,9 +489,10 @@
             q, grad = qbuf[rows, cols], og[rows, cols]
             k, v = kv[0, :n], kv[1, :n]
             scores = dot_nt(q, k)
-            q_pos = lax.broadcasted_iota(jnp.int32, (HD, n), 0) + i * HD
-            k_pos = lax.broadcasted_iota(jnp.int32, (HD, n), 1)
-            scores = jnp.where(k_pos <= q_pos, scores, -jnp.inf)
+            q_pos = lax.broadcasted_iota(jnp.int32, (HD, HD), 0)
+            k_pos = lax.broadcasted_iota(jnp.int32, (HD, HD), 1)
+            last = jnp.where(k_pos <= q_pos, scores[:, n - HD:], -jnp.inf)
+            scores = last if i == 0 else jnp.concatenate([scores[:, :n - HD], last], axis=1)
             expo = jnp.exp2((scores - jnp.max(scores, axis=-1, keepdims=True)) * (scale * LOG2E))
             probs = expo * (1.0 / jnp.sum(expo, axis=-1, keepdims=True))
             dprobs = dot_nt(grad, v)
@@ -504,7 +505,7 @@
             part[1, :n] += dot_tn(probs.astype(BF16), grad)
             return carry
 
-        lax.fori_loop(0, HEADS, head, 0, unroll=2 if i == 2 else 4)
+        lax.fori_loop(0, HEADS, head, 0, unroll=4)
         part_low[rows, :] = part[1 - role, rows, :].astype(BF16)
         send(("part", i), part_low.at[pl.ds(i * HD, HD)], part_in.at[pl.ds(i * HD, HD)], mate)
         if i == 1:

time: 139 us -> 138 us (level)
  no operation moved by 1% of the time
where the time goes in v5:
time: 138 us
  Pallas kernels  137 us (99%)
    pallas_call x1, Pallas kernels, body(): pl.pallas_call(kernel, out_shape=outs, in_specs=[anywhere] * 6, out_specs...  135 us

profile of v5, /device:TPU:1, one launch (start us, length us, event | category | flops | bytes accessed | tf_op | source)
XLA Modules:
  0.0 137.8 jit_solution(17494534221386572264)
XLA Ops:
  0.6 134.9 %attention_backward.1 = (bf16[384,512]{1,0:T(8,128)(2,1)}, bf16[512,512]{1,0:T(8,128)(2,1)}, bf16[512,128]{1,0:T(8,128)(2,1)}) custom-call(bf16[384,512]{1,0:T(8,128)(2,1)} %x_in.1, bf16[384,512]{1,0:T(8,128)(2,1)} %og_in.1, bf16[512,512]{1,0:T(8,128)(2,1)} %wq_in.1, bf16[512,128]{1,0:T(8,128)(2,1)} %wkv_in.1, f32[384,128]{1,0:T(8,128)} %constant.4.clone.cos_in, ...), custom_call_target="tpu_custom_call" | custom-call | tf_op jit(solution)/shard_map/attention_backward/pallas_call | solution.py:611
  135.6 2.1 %hand_on.1 = (bf16[384,512]{1,0:T(8,128)(2,1)}, bf16[512,512]{1,0:T(8,128)(2,1)}, bf16[512,128]{1,0:T(8,128)(2,1)}) custom-call(bf16[384,512]{1,0:T(8,128)(2,1)} %get-tuple-element.6.refs_0_, bf16[512,512]{1,0:T(8,128)(2,1)} %get-tuple-element.7.refs_1_, bf16[512,128]{1,0:T(8,128)(2,1)} %get-tuple-element.8.refs_2_), custom_call_target="tpu_custom_call" | custom-call | tf_op jit(solution)/shard_map/hand_on/pallas_call | solution.py:655

commit v6 on v5

--- a/solution.py
+++ b/solution.py
@@ -15,7 +15,7 @@
 CHUNKS = ((0, HD), (2 * HD, HD // 2))
 LAST = 32
 MOST = TOK - LAST
-N_SEMS = 166
+N_SEMS = 178
 N_SEND = 56
 LOG2E = float(np.log2(np.e))
 
@@ -181,12 +181,42 @@
         recv_w(("xmr", dz), wb(2, dz, 0), 1)
         send_w(("sfar", dz), wb(2, dz, 0), 1, sib)
 
+    def quarter(block, p):
+        return wbuf.at[block, pl.ds(p * (HW // 2), HW // 2)]
+
+    def send_q(name, block, p, to):
+        send((name, p), quarter(block, p), quarter(block, p), to)
+
+    def recv_q(name, block, p):
+        recv((name, p), quarter(block, p))
+
     def from_zl(h):
         block = wb(0, 1, 0)
         recv_w("zl", block, h)
-        send_w(("xp", 1), block, h, xp)
-        send_w(("xm", 1), block, h, xm)
+        for k in (0, 1):
+            send_q("xpq", block, 2 * h + k, xp)
+            send_q("xmq", block, 2 * h + 1 - k, xm)
         send_w("szl", block, h, sib)
+
+    def relay_q(h):
+        recv_q("xpq", wb(3, 1, 0), 2 * h)
+        send_q("xpqr", wb(3, 1, 0), 2 * h, xp)
+        recv_q("xmq", wb(1, 1, 0), 2 * h + 1)
+        send_q("xmqr", wb(1, 1, 0), 2 * h + 1, xm)
+        send_q("sxpq", wb(3, 1, 0), 2 * h, sib)
+        send_q("sxmq", wb(1, 1, 0), 2 * h + 1, sib)
+
+    def rest_q(h):
+        recv_q("xpq", wb(3, 1, 0), 2 * h + 1)
+        send_q("sxpq", wb(3, 1, 0), 2 * h + 1, sib)
+        recv_q("xmq", wb(1, 1, 0), 2 * h)
+        send_q("sxmq", wb(1, 1, 0), 2 * h, sib)
+
+    def far_q(h):
+        recv_q("xpqr", wb(2, 1, 0), 2 * h)
+        send_q("sfarq", wb(2, 1, 0), 2 * h, sib)
+        recv_q("xmqr", wb(2, 1, 0), 2 * h + 1)
+        send_q("sfarq", wb(2, 1, 0), 2 * h + 1, sib)
 
     acc[...] = jnp.zeros_like(acc)
     part[...] = jnp.zeros_like(part)
@@ -242,6 +272,7 @@
     far_x(0)
     from_zl(0)
     relay_y(3, 1)
+    relay_q(0)
     relay_y(1, 0)
     from_zl(1)
     rest_y(0)
@@ -255,32 +286,34 @@
     spread_y(2, 0)
     recv_x("zmr", tb(2, 0), 1)
     spread_y(2, 1)
+    rest_q(0)
+    far_q(0)
     project_row(0, 0)
-    relay_x(1, 0)
-    relay_x(1, 1)
     rest_y(3)
     far_y(3)
     project_row(3, 0)
+    relay_q(1)
     relay_y(2, 0)
     relay_y(2, 1)
     rest_y(1)
     far_y(1)
     project_row(1, 0)
-    rest_x(1)
+    rest_q(1)
     for h in (0, 1):
         recv_w("szl", wb(0, 1, 1), h)
-        recv_w(("sxp", 1), wb(3, 1, 1), h)
-        recv_w(("sxm", 1), wb(1, 1, 1), h)
+        for p in (2 * h, 2 * h + 1):
+            recv_q("sxpq", wb(3, 1, 1), p)
+            recv_q("sxmq", wb(1, 1, 1), p)
     project_row(0, 1)
-    far_x(1)
+    far_q(1)
     project_row(3, 1)
     project_row(1, 1)
     rest_y(2)
     far_y(2)
     project_row(2, 0, kv_cols)
     project_row(2, 1, kv_cols)
-    for h in (0, 1):
-        recv_w(("sfar", 1), wb(2, 1, 1), h)
+    for p in range(4):
+        recv_q("sfarq", wb(2, 1, 1), p)
     def last_two(cols):
         b0, b1 = wb(2, 1, 0), wb(2, 1, 1)
         acc[:, cols] += dot_nn(xbuf[b0], wbuf[b0, :, cols]) + dot_nn(xbuf[b1], wbuf[b1, :, cols])

time: 138 us -> 138 us (level)
  no operation moved by 1% of the time
where the time goes in v6:
time: 138 us; the launch traced here: 137 us
  Pallas kernels  136 us (99%)
    pallas_call x1, Pallas kernels, body(): pl.pallas_call(kernel, out_shape=outs, in_specs=[anywhere] * 6, out_specs...  134 us

profile of v6, /device:TPU:1, one launch (start us, length us, event | category | flops | bytes accessed | tf_op | source)
XLA Modules:
  0.0 137.2 jit_solution(16807595399303345913)
XLA Ops:
  0.6 134.3 %attention_backward.1 = (bf16[384,512]{1,0:T(8,128)(2,1)}, bf16[512,512]{1,0:T(8,128)(2,1)}, bf16[512,128]{1,0:T(8,128)(2,1)}) custom-call(bf16[384,512]{1,0:T(8,128)(2,1)} %x_in.1, bf16[384,512]{1,0:T(8,128)(2,1)} %og_in.1, bf16[512,512]{1,0:T(8,128)(2,1)} %wq_in.1, bf16[512,128]{1,0:T(8,128)(2,1)} %wkv_in.1, f32[384,128]{1,0:T(8,128)} %constant.4.clone.cos_in, ...), custom_call_target="tpu_custom_call" | custom-call | tf_op jit(solution)/shard_map/attention_backward/pallas_call | solution.py:644
  134.9 2.1 %hand_on.1 = (bf16[384,512]{1,0:T(8,128)(2,1)}, bf16[512,512]{1,0:T(8,128)(2,1)}, bf16[512,128]{1,0:T(8,128)(2,1)}) custom-call(bf16[384,512]{1,0:T(8,128)(2,1)} %get-tuple-element.6.refs_0_, bf16[512,512]{1,0:T(8,128)(2,1)} %get-tuple-element.7.refs_1_, bf16[512,128]{1,0:T(8,128)(2,1)} %get-tuple-element.8.refs_2_), custom_call_target="tpu_custom_call" | custom-call | tf_op jit(solution)/shard_map/hand_on/pallas_call | solution.py:688
